TPU v7x, 32 devices: a whole 2x2x4 slice. The times are simulated.
32 devices in a mesh: polar: 8 (over z, core), azimuth: 4 (over y, x).
Axes of the slice: x: 2, y: 2, z: 4, core: 2. Of those that a mesh axis runs over, the one named last changes fastest.
Arguments:
- signal: bfloat16 [512, 768, 256], P('polar', 'azimuth'), may hold values from -6 to 6
- cotangent: bfloat16 [512, 768, 256], P('polar', 'azimuth'), may hold values from -6 to 6
- mixing: bfloat16 [2, 256, 256], replicated, may hold values from -0.25 to 0.25
- coupling: bfloat16 [8, 6, 64, 64], replicated, may hold values from -0.75 to 0.75
- filters: float32 [8, 6, 2, 384], P(None, None, None, 'azimuth'), may hold values from -4 to 4
- band_counts: int32 [8], replicated, may hold values from 2 to 6, as said below
- band_offsets: int32 [8, 6], replicated, may hold values from -1 to 1, as said below
- band_basis: int32 [8, 6], replicated, may hold values from 0 to 1
Outputs:
- output: bfloat16 [512, 768, 256], P('polar', 'azimuth')
- signal_grad: bfloat16 [512, 768, 256], P('polar', 'azimuth')
Inputs may be any that keep to these rules, and one draw needn't show every extreme that they name: `band_counts`: blocks 1 and 6 use all 6 slots; the two end blocks use at most 4. `band_offsets`: for every block b, the first band_counts[b] slots name distinct pairs of offset and basis, and b plus the offset lies in 0 to 7; later slots are unused.
All inputs are finite; a program needn't handle non-finite values.
Results may differ from a plain program's by a relative error of at most 0.0075.
Values may be sent and summed in bfloat16 or wider, within the bound.
A program may use at most 192 MiB of HBM per device.

v0:
```python
import math

import jax
import jax.numpy as jnp
from jax import lax
from jax.sharding import PartitionSpec as P

NLON = 768
M = 384
K = 2
BLOCK = 64


def extended(cells, sides, width):
    for axis, dim in sides:
        count = lax.axis_size(axis)
        ends = count - 1
        head = lax.slice_in_dim(cells, 0, width, axis=dim)
        tail = lax.slice_in_dim(cells, cells.shape[dim] - width, cells.shape[dim], axis=dim)
        cells = jnp.concatenate(
            [
                lax.ppermute(tail, axis, [(i, (i + 1) % count) for i in range(ends)]),
                cells,
                lax.ppermute(head, axis, [((i + 1) % count, i) for i in range(ends)]),
            ],
            axis=dim,
        )
    return cells


def spectral_tables():
    longitude = jnp.arange(NLON, dtype=jnp.int32)
    wavenumber = jnp.arange(M, dtype=jnp.int32)
    product_mod = longitude[:, None] * wavenumber[None, :] % NLON
    phase_angle = product_mod.astype(jnp.float32) * (2.0 * math.pi / NLON)
    cosine = jnp.cos(phase_angle)
    sine_part = jnp.sin(phase_angle)
    forward = jnp.stack([cosine, -sine_part], axis=1).astype(jnp.bfloat16)
    weight = jnp.where(wavenumber == 0, 1.0, 2.0).astype(jnp.float32) / NLON
    inverse = jnp.transpose(
        jnp.stack([cosine, -sine_part], axis=0) * weight[None, None, :], (2, 0, 1)
    ).astype(jnp.bfloat16)
    return (forward, inverse)


def apply_filter(filt, coupled, conjugate):
    real_part = filt[0][:, None, None]
    imag_part = filt[1][:, None, None]
    if conjugate:
        imag_part = -imag_part
    leading = real_part * coupled[:, 0] - imag_part * coupled[:, 1]
    trailing = real_part * coupled[:, 1] + imag_part * coupled[:, 0]
    return jnp.stack([leading, trailing], axis=1)


def rows_of(rims, member, start_row):
    mode_local = rims.shape[0]
    piece = lax.dynamic_slice(
        rims, (0, member, 0, start_row, 0), (mode_local, 1, 2, BLOCK, rims.shape[4])
    )
    return piece[:, 0]


def per_device(signal, cotangent, mixing, coupling, filters, band_counts, band_offsets, band_basis):
    forward, inverse = spectral_tables()
    mode_local = filters.shape[3]
    blocks = lax.axis_size("polar")
    own_block = lax.axis_index("polar")
    inputs = (signal, cotangent)
    leading = jnp.einsum(
        "inc,npm->mpic",
        lax.all_to_all(inputs[0], "azimuth", split_axis=2, concat_axis=1, tiled=True),
        forward,
        preferred_element_type=jnp.float32,
    )
    trailing = jnp.einsum(
        "inc,mpn->mpic",
        lax.all_to_all(inputs[1], "azimuth", split_axis=2, concat_axis=1, tiled=True),
        inverse,
        preferred_element_type=jnp.float32,
    )
    stacked = jnp.stack([leading, trailing], axis=1).astype(jnp.bfloat16)
    both_spectra = lax.all_to_all(stacked, "azimuth", split_axis=0, concat_axis=4, tiled=True)
    rims = extended(both_spectra, (("polar", 3),), BLOCK)
    channels = signal.shape[2]
    zero_sum = jnp.zeros((mode_local, 2, BLOCK, channels), jnp.float32)
    slot_count = coupling.shape[1]

    def forward_basis(basis_index):

        def forward_slot(slot, running):
            used = band_basis[own_block, slot] == basis_index

            def forward_update(running):
                offset = band_offsets[own_block, slot]
                source = rows_of(rims, 0, (offset + 1) * BLOCK)
                coupled = jnp.einsum(
                    "rj,mpjc->mprc",
                    coupling[own_block, slot],
                    source,
                    preferred_element_type=jnp.float32,
                )
                return running + apply_filter(filters[own_block, slot], coupled, False)

            return lax.cond(used, forward_update, lambda kept: kept, running)

        return lax.fori_loop(0, band_counts[own_block], forward_slot, zero_sum).astype(jnp.bfloat16)

    basis_rounded = jnp.stack([forward_basis(index) for index in range(K)], axis=0)
    out_spectra = jnp.einsum(
        "kmpic,kcd->mpid", basis_rounded, mixing, preferred_element_type=jnp.float32
    ).astype(jnp.bfloat16)

    def backward_basis(basis_index):
        running = zero_sum
        for step_by in (-1, 0, 1):
            neighbour = own_block + step_by
            inside = (neighbour >= 0) & (neighbour < blocks)
            safe = jnp.clip(neighbour, 0, blocks - 1)
            source = rows_of(rims, 1, (step_by + 1) * BLOCK)
            count_there = band_counts[safe]

            def backward_slot(
                slot,
                running,
                safe=safe,
                inside=inside,
                source=source,
                count_there=count_there,
                step_by=step_by,
            ):
                used = (
                    inside
                    & (slot < count_there)
                    & (band_offsets[safe, slot] == -step_by)
                    & (band_basis[safe, slot] == basis_index)
                )

                def backward_update(running):
                    lifted = jnp.einsum(
                        "jr,mpjc->mprc",
                        coupling[safe, slot],
                        source,
                        preferred_element_type=jnp.float32,
                    )
                    return running + apply_filter(filters[safe, slot], lifted, True)

                return lax.cond(used, backward_update, lambda kept: kept, running)

            running = lax.fori_loop(0, slot_count, backward_slot, running)
        return running.astype(jnp.bfloat16)

    back_rounded = jnp.stack([backward_basis(index) for index in range(K)], axis=0)
    grad_spectra = jnp.einsum(
        "kmpjd,kcd->mpjc", back_rounded, mixing, preferred_element_type=jnp.float32
    ).astype(jnp.bfloat16)
    stacked = jnp.stack([out_spectra, grad_spectra], axis=1)
    piece = lax.all_to_all(stacked, "azimuth", split_axis=4, concat_axis=0, tiled=True)
    leading = jnp.einsum("mpic,mpn->inc", piece[:, 0], inverse, preferred_element_type=jnp.float32)
    trailing = jnp.einsum("mpjc,npm->jnc", piece[:, 1], forward, preferred_element_type=jnp.float32)
    columns = jnp.stack([leading, trailing], axis=0).astype(jnp.bfloat16)
    result = lax.all_to_all(columns, "azimuth", split_axis=2, concat_axis=3, tiled=True)
    return (result[0], result[1])


def solution(mesh):
    return jax.shard_map(
        per_device,
        mesh=mesh,
        in_specs=(
            P("polar", "azimuth", None),
            P("polar", "azimuth", None),
            P(),
            P(),
            P(None, None, None, "azimuth"),
            P(),
            P(),
            P(),
        ),
        out_specs=(P("polar", "azimuth", None), P("polar", "azimuth", None)),
        check_vma=False,
    )
```

profile of v0, /device:TPU:1, one launch (start us, length us, event | category | flops | bytes accessed | tf_op | source)
XLA Modules:
  0.0 1811.2 jit_solution(2552373354926480932)
XLA Ops:
  0.6 12.2 copy.78
  18.5 12.2 copy.75
  30.6 80.5 %all-to-all-done.1 = bf16[64,192,256]{1,0,2:T(8,128)(2,1)} async-done(((bf16[64,192,256]{1,0,2:T(8,128)(2,1)}), bf16[64,192,256]{1,0,2:T(8,128)(2,1)}, u32[]{:S(2)}, u32[]{:S(2)}) %all-to-all-start.1) | async-done | bytes 6291488 | tf_op jit(solution)/shard_map/all_to_all | solution.py:78
  128.6 12.5 copy.80
  141.1 14.9 reshape.267
  156.0 52.6 %all-to-all-done = bf16[64,192,256]{1,0,2:T(8,128)(2,1)} async-done(((bf16[64,192,256]{1,0,2:T(8,128)(2,1)}), bf16[64,192,256]{1,0,2:T(8,128)(2,1)}, u32[]{:S(2)}, u32[]{:S(2)}) %all-to-all-start) | async-done | bytes 6291488 | tf_op jit(solution)/shard_map/all_to_all | solution.py:72
  208.6 12.1 copy.77
  220.7 15.0 reshape.265
  255.2 35.0 %copy.81 = bf16[384,2,2,64,64]{4,3,2,1,0:T(8,128)(2,1)} copy(bf16[384,2,2,64,64]{0,4,3,2,1:T(8,128)(2,1)} %pad_maximum_fusion.1) | data formatting | bytes 25165824 | tf_op jit(solution)/shard_map/stack | solution.py:82
  290.3 37.3 %reshape.275 = bf16[4,2,786432]{2,1,0:T(2,128)(2,1)} reshape(bf16[384,2,2,64,64]{4,3,2,1,0:T(8,128)(2,1)} %copy.81) | data formatting | bytes 25165824
  327.6 145.1 %all_to_all.87 = bf16[4,2,786432]{2,1,0:T(2,128)(2,1)} all-to-all(bf16[4,2,786432]{2,1,0:T(2,128)(2,1)} %reshape.275), channel_id=1, replica_groups=mesh['polar'=8,'azimuth'=4] {'azimuth'}, dimensions={0} | all-to-all | bytes 25165824 | tf_op jit(solution)/shard_map/all_to_all | solution.py:83
  472.6 36.7 %reshape.276 = bf16[384,2,2,64,64]{4,3,2,1,0:T(8,128)(2,1)} reshape(bf16[4,2,786432]{2,1,0:T(2,128)(2,1)} %all_to_all.87) | data formatting | bytes 25165824
  509.4 31.2 %copy.82 = bf16[4,96,2,2,64,64]{1,5,0,4,3,2:T(8,128)(2,1)} copy(bf16[4,96,2,2,64,64]{5,4,3,2,1,0:T(8,128)(2,1)} %bitcast.283) | data formatting | bytes 25165824 | tf_op jit(solution)/shard_map/all_to_all | solution.py:83
  540.6 21.8 %copy.83 = bf16[96,2,2,64,256]{4,3,2,1,0:T(8,128)(2,1)} copy(bf16[96,2,2,64,256]{0,4,3,2,1:T(8,128)(2,1)} %bitcast.280) | data formatting | bytes 25165824 | tf_op jit(solution)/shard_map/all_to_all | solution.py:83
  593.5 110.5 %collective-permute-done = bf16[96,2,2,64,256]{4,3,2,1,0:T(8,128)(2,1)} collective-permute-done((bf16[96,2,2,64,256]{4,3,2,1,0:T(8,128)(2,1)}, bf16[96,2,2,64,256]{4,3,2,1,0:T(8,128)(2,1)}, u32[]{:S(2)}, u32[]{:S(2)}) %collective-permute-start) | collective-permute-done | bytes 12582944 | tf_op jit(solution)/shard_map/ppermute | solution.py:22
  716.8 38.9 %while.149 = (s32[]{:T(128)}, f32[96,2,64,256]{3,2,1,0:T(8,128)}, s32[]{:T(128)}, pred[]{:T(512)}, s32[8,6]{1,0:T(8,128)S(1)}, /*index=5*/s32[]{:T(128)}, s32[8,...) while((s32[]{:T(128)}, f32[96,2,64,256]{3,2,1,0:T(8,128)}, ...), condition=%wide.region_23.24_spmd, body=%wide.region_20.23_spmd.sunk | while | flops 418381920 | bytes 81809480 | solution.py:150
  723.2 19.6 %conditional.21 = (f32[96,2,64,256]{3,2,1,0:T(8,128)}) conditional(s32[]{:T(128)} %convert_element_type.190, f32[96,2,64,256]{3,2,1,0:T(8,128)} %get-tuple-element.3049, (s32[]{:T(128)}, s32[]{:T(128)}, f32[8,6,2,96]{3,2,1,0:T(2,128)}, bf16[8,6,64,64]{2,3,1,0:T(8,128)(2,1)S(1)}, bf16[96,2,64,256]{3,2,1,0:T(8,128)(2,1)}, ...), branch_computations={%region_21.21_spmd, %region_22.22_spmd} | conditional | flops 418381920 | bytes 81809240 | solution.py:148
  755.7 38.4 %while.150 = (s32[]{:T(128)}, f32[96,2,64,256]{3,2,1,0:T(8,128)}, s32[]{:T(128)}, pred[]{:T(512)}, s32[8,6]{1,0:T(8,128)S(1)}, /*index=5*/s32[]{:T(128)}, s32[8,...) while((s32[]{:T(128)}, f32[96,2,64,256]{3,2,1,0:T(8,128)}, ...), condition=%wide.region_27.28_spmd, body=%wide.region_24.27_spmd.sunk | while | flops 418381920 | bytes 81809488 | solution.py:150
  768.2 19.6 %conditional.22 = (f32[96,2,64,256]{3,2,1,0:T(8,128)}) conditional(s32[]{:T(128)} %convert_element_type.191, f32[96,2,64,256]{3,2,1,0:T(8,128)} %get-tuple-element.3086, (s32[]{:T(128)}, s32[]{:T(128)}, f32[8,6,2,96]{3,2,1,0:T(2,128)}, bf16[8,6,64,64]{2,3,1,0:T(8,128)(2,1)S(1)}, bf16[96,2,64,256]{3,2,1,0:T(8,128)(2,1)}, ...), branch_computations={%region_25.25_spmd, %region_26.26_spmd} | conditional | flops 418381920 | bytes 81809240 | solution.py:148
  800.7 40.5 %while.151 = (s32[]{:T(128)}, f32[96,2,64,256]{3,2,1,0:T(8,128)}, s32[]{:T(128)}, pred[]{:T(512)}, s32[8,6]{1,0:T(8,128)S(1)}, /*index=5*/s32[]{:T(128)}, s32[8,...) while((s32[]{:T(128)}, f32[96,2,64,256]{3,2,1,0:T(8,128)}, ...), condition=%wide.region_31.32_spmd, body=%wide.region_28.31_spmd.sunk | while | flops 418381920 | bytes 81809488 | solution.py:150
  807.8 19.6 %conditional.23 = (f32[96,2,64,256]{3,2,1,0:T(8,128)}) conditional(s32[]{:T(128)} %convert_element_type.192, f32[96,2,64,256]{3,2,1,0:T(8,128)} %get-tuple-element.3125, (s32[]{:T(128)}, s32[]{:T(128)}, f32[8,6,2,96]{3,2,1,0:T(2,128)}, bf16[8,6,64,64]{2,3,1,0:T(8,128)(2,1)S(1)}, bf16[96,2,64,256]{3,2,1,0:T(8,128)(2,1)}, ...), branch_computations={%region_29.29_spmd, %region_30.30_spmd} | conditional | flops 418381920 | bytes 81809240 | solution.py:148
  855.5 40.1 %while.146 = (s32[]{:T(128)}, f32[96,2,64,256]{3,2,1,0:T(8,128)}, s32[]{:T(128)}, pred[]{:T(512)}, s32[8,6]{1,0:T(8,128)S(1)}, /*index=5*/s32[]{:T(128)}, s32[8,...) while((s32[]{:T(128)}, f32[96,2,64,256]{3,2,1,0:T(8,128)}, ...), condition=%wide.region_11.12_spmd, body=%wide.region_8.11_spmd.sunk | while | flops 418381920 | bytes 81809488 | solution.py:150
  865.7 19.7 %conditional.18 = (f32[96,2,64,256]{3,2,1,0:T(8,128)}) conditional(s32[]{:T(128)} %convert_element_type.187, f32[96,2,64,256]{3,2,1,0:T(8,128)} %get-tuple-element.3164, (s32[]{:T(128)}, s32[]{:T(128)}, f32[8,6,2,96]{3,2,1,0:T(2,128)}, bf16[8,6,64,64]{2,3,1,0:T(8,128)(2,1)S(1)}, bf16[96,2,64,256]{3,2,1,0:T(8,128)(2,1)}, ...), branch_computations={%region_9.9_spmd, %region_10.10_spmd} | conditional | flops 418381920 | bytes 81809240 | solution.py:148
  895.6 39.0 %while.147 = (s32[]{:T(128)}, f32[96,2,64,256]{3,2,1,0:T(8,128)}, s32[]{:T(128)}, pred[]{:T(512)}, s32[8,6]{1,0:T(8,128)S(1)}, /*index=5*/s32[]{:T(128)}, s32[8,...) while((s32[]{:T(128)}, f32[96,2,64,256]{3,2,1,0:T(8,128)}, ...), condition=%wide.region_15.16_spmd, body=%wide.region_12.15_spmd.sunk | while | flops 418381920 | bytes 81809480 | solution.py:150
  905.5 19.7 %conditional.19 = (f32[96,2,64,256]{3,2,1,0:T(8,128)}) conditional(s32[]{:T(128)} %convert_element_type.188, f32[96,2,64,256]{3,2,1,0:T(8,128)} %get-tuple-element.3202, (s32[]{:T(128)}, s32[]{:T(128)}, f32[8,6,2,96]{3,2,1,0:T(2,128)}, bf16[8,6,64,64]{2,3,1,0:T(8,128)(2,1)S(1)}, bf16[96,2,64,256]{3,2,1,0:T(8,128)(2,1)}, ...), branch_computations={%region_13.13_spmd, %region_14.14_spmd} | conditional | flops 418381920 | bytes 81809240 | solution.py:148
  934.6 19.2 %while.148 = (s32[]{:T(128)}, f32[96,2,64,256]{3,2,1,0:T(8,128)}, s32[]{:T(128)}, pred[]{:T(512)}, s32[8,6]{1,0:T(8,128)S(1)}, /*index=5*/s32[]{:T(128)}, s32[8,...) while((s32[]{:T(128)}, f32[96,2,64,256]{3,2,1,0:T(8,128)}, ...), condition=%wide.region_19.20_spmd, body=%wide.region_16.19_spmd.sunk | while | flops 418381920 | bytes 81809488 | solution.py:150
  962.2 21.6 %copy.86 = bf16[96,2,2,64,256]{0,4,3,2,1:T(8,128)(2,1)} copy(bf16[96,2,2,64,256]{4,3,2,1,0:T(8,128)(2,1)} %collective-permute-done.1) | data formatting | bytes 25165824 | tf_op jit(solution)/shard_map/ppermute | solution.py:24
  983.7 21.6 %copy.85 = bf16[96,2,2,64,256]{0,4,3,2,1:T(8,128)(2,1)} copy(bf16[96,2,2,64,256]{4,3,2,1,0:T(8,128)(2,1)} %collective-permute-done) | data formatting | bytes 25165824 | tf_op jit(solution)/shard_map/ppermute | solution.py:22
  1005.3 33.5 %pad_maximum_fusion = bf16[96,2,2,192,256]{0,4,3,2,1:T(8,128)(2,1)} fusion(bf16[96,2,2,64,256]{0,4,3,2,1:T(8,128)(2,1)} %copy.86, bf16[96,2,2,64,256]{0,4,3,2,1:T(8,128)(2,1)} %bitcast.282, bf16[96,2,2,64,256]{0,4,3,2,1:T(8,128)(2,1)} %copy.85), kind=kLoop, calls=%fused_computation.86 | loop fusion | flops 37748736 | bytes 75497472 | tf_op jit(solution)/shard_map/concatenate | solution.py:20
  1038.9 57.6 %copy.87 = bf16[96,2,2,192,256]{4,3,2,0,1:T(8,128)(2,1)} copy(bf16[96,2,2,192,256]{0,4,3,2,1:T(8,128)(2,1)} %pad_maximum_fusion) | data formatting | bytes 75497472 | tf_op jit(solution)/shard_map/while | solution.py:107
  1102.6 75.0 %while.145 = (s32[]{:T(128)}, f32[96,2,64,256]{3,2,1,0:T(8,128)}, s32[]{:T(128)}, s32[8,6]{1,0:T(8,128)S(1)}, s32[]{:T(128)}, /*index=5*/s32[]{:T(128)}, f32[8,6...) while((s32[]{:T(128)}, f32[96,2,64,256]{3,2,1,0:T(8,128)}, ...), condition=%wide.region_7.8_spmd, body=%wide.region_4.7_spmd.sunk | while | flops 418381824 | bytes 81809576 | solution.py:107
  1106.3 21.1 %conditional.17 = (f32[96,2,64,256]{3,2,1,0:T(8,128)}) conditional(s32[]{:T(128)} %bitcast.267, f32[96,2,64,256]{3,2,1,0:T(8,128)} %get-tuple-element.3279, (s32[]{:T(128)}, s32[]{:T(128)}, f32[8,6,2,96]{3,2,1,0:T(2,128)}, s32[8,6]{1,0:T(8,128)S(1)}, bf16[96,2,2,192,256]{4,3,2,0,1:T(8,128)(2,1)}, /*index=5*/bf16[8,6,64,64]{3,2,1,0:T(8,128)(2,1)}, ...), branch_computations={%region_5.5_spmd, %region_6.6_spmd} | conditional | flops 418381824 | bytes 81809320 | solution.py:105
  1131.0 21.1 %conditional.17 = (f32[96,2,64,256]{3,2,1,0:T(8,128)}) conditional(s32[]{:T(128)} %bitcast.267, f32[96,2,64,256]{3,2,1,0:T(8,128)} %get-tuple-element.3279, (s32[]{:T(128)}, s32[]{:T(128)}, f32[8,6,2,96]{3,2,1,0:T(2,128)}, s32[8,6]{1,0:T(8,128)S(1)}, bf16[96,2,2,192,256]{4,3,2,0,1:T(8,128)(2,1)}, /*index=5*/bf16[8,6,64,64]{3,2,1,0:T(8,128)(2,1)}, ...), branch_computations={%region_5.5_spmd, %region_6.6_spmd} | conditional | flops 418381824 | bytes 81809320 | solution.py:105
  1153.9 21.1 %conditional.17 = (f32[96,2,64,256]{3,2,1,0:T(8,128)}) conditional(s32[]{:T(128)} %bitcast.267, f32[96,2,64,256]{3,2,1,0:T(8,128)} %get-tuple-element.3279, (s32[]{:T(128)}, s32[]{:T(128)}, f32[8,6,2,96]{3,2,1,0:T(2,128)}, s32[8,6]{1,0:T(8,128)S(1)}, bf16[96,2,2,192,256]{4,3,2,0,1:T(8,128)(2,1)}, /*index=5*/bf16[8,6,64,64]{3,2,1,0:T(8,128)(2,1)}, ...), branch_computations={%region_5.5_spmd, %region_6.6_spmd} | conditional | flops 418381824 | bytes 81809320 | solution.py:105
  1192.1 75.6 %while.144 = (s32[]{:T(128)}, f32[96,2,64,256]{3,2,1,0:T(8,128)}, s32[]{:T(128)}, s32[8,6]{1,0:T(8,128)S(1)}, s32[]{:T(128)}, /*index=5*/s32[]{:T(128)}, f32[8,6...) while((s32[]{:T(128)}, f32[96,2,64,256]{3,2,1,0:T(8,128)}, ...), condition=%wide.region_3.4_spmd, body=%wide.region_0.3_spmd.sunk | while | flops 418381824 | bytes 81809576 | solution.py:107
  1194.1 21.0 %conditional.16 = (f32[96,2,64,256]{3,2,1,0:T(8,128)}) conditional(s32[]{:T(128)} %bitcast.266, f32[96,2,64,256]{3,2,1,0:T(8,128)} %get-tuple-element.3321, (s32[]{:T(128)}, s32[]{:T(128)}, f32[8,6,2,96]{3,2,1,0:T(2,128)}, s32[8,6]{1,0:T(8,128)S(1)}, bf16[96,2,2,192,256]{4,3,2,0,1:T(8,128)(2,1)}, /*index=5*/bf16[8,6,64,64]{3,2,1,0:T(8,128)(2,1)}, ...), branch_computations={%region_1.1_spmd, %region_2.2_spmd} | conditional | flops 418381824 | bytes 81809320 | solution.py:105
  1219.1 21.0 %conditional.16 = (f32[96,2,64,256]{3,2,1,0:T(8,128)}) conditional(s32[]{:T(128)} %bitcast.266, f32[96,2,64,256]{3,2,1,0:T(8,128)} %get-tuple-element.3321, (s32[]{:T(128)}, s32[]{:T(128)}, f32[8,6,2,96]{3,2,1,0:T(2,128)}, s32[8,6]{1,0:T(8,128)S(1)}, bf16[96,2,2,192,256]{4,3,2,0,1:T(8,128)(2,1)}, /*index=5*/bf16[8,6,64,64]{3,2,1,0:T(8,128)(2,1)}, ...), branch_computations={%region_1.1_spmd, %region_2.2_spmd} | conditional | flops 418381824 | bytes 81809320 | solution.py:105
  1246.1 21.0 %conditional.16 = (f32[96,2,64,256]{3,2,1,0:T(8,128)}) conditional(s32[]{:T(128)} %bitcast.266, f32[96,2,64,256]{3,2,1,0:T(8,128)} %get-tuple-element.3321, (s32[]{:T(128)}, s32[]{:T(128)}, f32[8,6,2,96]{3,2,1,0:T(2,128)}, s32[8,6]{1,0:T(8,128)S(1)}, bf16[96,2,2,192,256]{4,3,2,0,1:T(8,128)(2,1)}, /*index=5*/bf16[8,6,64,64]{3,2,1,0:T(8,128)(2,1)}, ...), branch_computations={%region_1.1_spmd, %region_2.2_spmd} | conditional | flops 418381824 | bytes 81809320 | solution.py:105
  1297.6 24.3 %copy.97 = bf16[96,2,2,64,256]{0,3,2,1,4:T(8,128)(2,1)} copy(bf16[96,2,2,64,256]{4,3,2,0,1:T(8,128)(2,1)} %pad_maximum_fusion.2) | data formatting | bytes 25165824 | tf_op jit(solution)/shard_map/stack | solution.py:157
  1321.9 152.9 %all_to_all.88 = bf16[96,2,2,64,256]{0,3,2,1,4:T(8,128)(2,1)S(1)} all-to-all(bf16[96,2,2,64,256]{0,3,2,1,4:T(8,128)(2,1)} %copy.97), channel_id=1, replica_groups=mesh['polar'=8,'azimuth'=4] {'azimuth'}, dimensions={4} | all-to-all | bytes 25165824 | tf_op jit(solution)/shard_map/all_to_all | solution.py:158
  1474.8 36.1 %copy.99 = bf16[4,96,2,2,64,64]{1,0,5,3,4,2:T(4,128)(2,1)} copy(bf16[4,96,2,2,64,64]{1,4,3,2,5,0:T(8,128)(2,1)S(1)} %bitcast.287) | data formatting | bytes 25165824 | tf_op jit(solution)/shard_map/all_to_all | solution.py:158
  1510.9 26.3 %all_to_all.78 = bf16[384,2,2,64,64]{0,4,2,3,1:T(8,128)(2,1)} reshape(bf16[4,96,2,2,64,64]{1,0,5,3,4,2:T(4,128)(2,1)} %copy.99) | data formatting | bytes 25165824 | tf_op jit(solution)/shard_map/all_to_all | solution.py:158
  1558.0 35.0 %copy.100 = bf16[2,64,768,64]{3,1,0,2:T(8,128)(2,1)} copy(bf16[2,64,768,64]{2,3,1,0:T(8,128)(2,1)} %pad_maximum_fusion.3) | data formatting | bytes 25165824 | tf_op jit(solution)/shard_map/stack | solution.py:161
  1592.9 37.5 %reshape.277 = bf16[4,2,786432]{2,1,0:T(2,128)(2,1)} reshape(bf16[768,2,64,64]{3,2,1,0:T(8,128)(2,1)} %bitcast.284) | data formatting | bytes 25165824
  1630.5 79.9 %all_to_all.89 = bf16[4,2,786432]{2,1,0:T(2,128)(2,1)} all-to-all(bf16[4,2,786432]{2,1,0:T(2,128)(2,1)} %reshape.277), channel_id=1, replica_groups=mesh['polar'=8,'azimuth'=4] {'azimuth'}, dimensions={0} | all-to-all | bytes 25165824 | tf_op jit(solution)/shard_map/all_to_all | solution.py:162
  1710.4 36.7 %reshape.278 = bf16[768,2,64,64]{3,2,1,0:T(8,128)(2,1)} reshape(bf16[4,2,786432]{2,1,0:T(2,128)(2,1)} %all_to_all.89) | data formatting | bytes 25165824
  1747.1 31.3 %copy.101 = bf16[2,64,4,192,64]{3,4,2,1,0:T(8,128)(2,1)} copy(bf16[2,64,4,192,64]{4,1,0,3,2:T(8,128)(2,1)} %bitcast.285) | data formatting | bytes 25165824 | tf_op jit(solution)/shard_map/all_to_all | solution.py:162
  1778.4 11.9 fusion.78
  (253 shorter events, 481.5 us)
Async XLA Ops:
  0.6 1275.4 %copy-start = (bf16[2,256,256]{2,1,0:T(8,128)(2,1)S(1)}, bf16[2,256,256]{2,1,0:T(8,128)(2,1)}, u32[]{:S(2)}) copy-start(bf16[2,256,256]{2,1,0:T(8,128)(2,1)} %param.42) | copy-start | bytes 786436
  12.8 98.3 %all-to-all-start.1 = ((bf16[64,192,256]{1,0,2:T(8,128)(2,1)}), bf16[64,192,256]{1,0,2:T(8,128)(2,1)}, u32[]{:S(2)}, u32[]{:S(2)}) async-start(bf16[64,192,256]{1,0,2:T(8,128)(2,1)} %copy.78), calls=%async_computation.1 | async-start | bytes 16777216 | tf_op jit(solution)/shard_map/all_to_all | solution.py:78
  111.2 97.4 %all-to-all-start = ((bf16[64,192,256]{1,0,2:T(8,128)(2,1)}), bf16[64,192,256]{1,0,2:T(8,128)(2,1)}, u32[]{:S(2)}, u32[]{:S(2)}) async-start(bf16[64,192,256]{1,0,2:T(8,128)(2,1)} %copy.75), calls=%async_computation | async-start | bytes 16777216 | tf_op jit(solution)/shard_map/all_to_all | solution.py:72
  116.8 126.5 %copy-start.12 = (f32[384]{0:T(512)}, f32[384]{0:T(512)S(1)}, u32[]{:S(2)}) copy-start(f32[384]{0:T(512)S(1)} %select_multiply_fusion) | copy-start | bytes 4612
  128.6 114.8 %copy-start.3 = (f32[1,768,384]{1,2,0:T(8,128)}, f32[1,768,384]{1,2,0:T(8,128)S(1)}, u32[]{:S(2)}) copy-start(f32[1,768,384]{1,2,0:T(8,128)S(1)} %get-tuple-element.2542) | copy-start | bytes 3538948
  220.7 22.7 %slice-start = ((s8[6291456]{0:T(1024)(128)(4,1)}), s8[2097152]{0:T(1024)(128)(4,1)S(1)}, s32[]{:S(2)}) async-start(s8[6291456]{0:T(1024)(128)(4,1)} %bitcast.290), calls=%async_computation.5 | async-start | bytes 4194304
  235.7 7.7 slice-start.1
  235.7 7.7 copy-start.5
  540.6 32.5 %copy-start.6 = (bf16[8,6,64,64]{3,2,1,0:T(8,128)(2,1)S(1)}, bf16[8,6,64,64]{3,2,1,0:T(8,128)(2,1)}, u32[]{:S(2)}) copy-start(bf16[8,6,64,64]{3,2,1,0:T(8,128)(2,1)} %param.43) | copy-start | bytes 1179652
  540.6 32.9 %copy-start.11 = (s32[8]{0:T(128)S(1)}, s32[8]{0:T(128)}, u32[]{:S(2)}) copy-start(s32[8]{0:T(128)} %param.45) | copy-start | bytes 100
  562.4 141.6 %collective-permute-start = (bf16[96,2,2,64,256]{4,3,2,1,0:T(8,128)(2,1)}, bf16[96,2,2,64,256]{4,3,2,1,0:T(8,128)(2,1)}, u32[]{:S(2)}, u32[]{:S(2)}) collective-permute-start(bf16[96,2,2,64,256]{4,3,2,1,0:T(8,128)(2,1)} %copy.83), channel_id=1, source_target_pairs={{0,4},{4,8},{8,12},{12,16},{16,20},{20,24},{24,28},{1,5},{5,9},{9,... | collective-permute-start | bytes 37748744 | tf_op jit(solution)/shard_map/ppermute | solution.py:22
  568.4 225.7 %collective-permute-start.1 = (bf16[96,2,2,64,256]{4,3,2,1,0:T(8,128)(2,1)}, bf16[96,2,2,64,256]{4,3,2,1,0:T(8,128)(2,1)}, u32[]{:S(2)}, u32[]{:S(2)}) collective-permute-start(bf16[96,2,2,64,256]{4,3,2,1,0:T(8,128)(2,1)} %copy.83), channel_id=1, source_target_pairs={{4,0},{8,4},{12,8},{16,12},{20,16},{24,20},{28,24},{5,1},{9,5},{13... | collective-permute-start | bytes 37748744 | tf_op jit(solution)/shard_map/ppermute | solution.py:24
  710.6 6.1 copy-start.9
  710.6 6.1 copy-start.10
  1267.7 15.1 slice-start.2
  1276.0 6.8 slice-start.3
  1276.0 7.8 copy-start.2
  1510.9 26.3 %copy-start.7 = (bf16[768,1,384]{2,0,1:T(8,128)(2,1)S(1)}, bf16[768,1,384]{2,0,1:T(8,128)(2,1)}, u32[]{:S(2)}) copy-start(bf16[768,1,384]{2,0,1:T(8,128)(2,1)} %get-tuple-element.2544) | copy-start | bytes 1769476
  1510.9 26.3 %copy-start.8 = (bf16[768,1,384]{2,0,1:T(8,128)(2,1)S(1)}, bf16[768,1,384]{2,0,1:T(8,128)(2,1)}, u32[]{:S(2)}) copy-start(bf16[768,1,384]{2,0,1:T(8,128)(2,1)} %get-tuple-element.2545) | copy-start | bytes 1769476
  1537.2 8.5 copy-start.1
  1537.2 8.5 copy-start.4
  1537.2 8.5 copy-start.13
where the time goes:
time: 1820 us; the launch traced here: 1810 us
  local copies, waits for them, and re-layouts  726 us (40%)
  blocking collectives  378 us (21%)
  other arithmetic  257 us (14%)
  waiting for transfers between devices  244 us (13%)
  loops' own time  92.9 us (5%)
  matrix products  91.3 us (5%)
  starting transfers between devices  21.9 us (1%)
    unnamed x44, local copies, waits for them, and re-layouts  194 us
    all_to_all x1, blocking collectives, per_device(): lax.all_to_all(stacked, 'azimuth', split_axis=4, concat_axis=0, tiled=True)  153 us
    all_to_all x1, blocking collectives, per_device(): lax.all_to_all(stacked, 'azimuth', split_axis=0, concat_axis=4, tiled=True)  145 us
    ppermute x1, waiting for transfers between devices, extended(): lax.ppermute(tail, axis, [(i, (i + 1) % count) for i in range(ends)])  110 us
    all_to_all x1, waiting for transfers between devices, per_device(): lax.all_to_all(inputs[1], 'azimuth', split_axis=2, concat_axis=1, tiled=T...  80.5 us
    all_to_all x1, blocking collectives, per_device(): lax.all_to_all(columns, 'azimuth', split_axis=2, concat_axis=3, tiled=True)  79.9 us
    another operation x6, loops' own time, backward_basis(): running = lax.fori_loop(0, slot_count, backward_slot, running)  71.2 us
    add x6, other arithmetic, forward_update(): return running + apply_filter(filters[own_block, slot], coupled, False)  66.8 us
  transfers between devices with their start and end apart: 4, of which 3 were waited for; matrix products, arithmetic and copies ran while one was open for 8% of the time, Pallas kernels for 0%

commit v1 on v0

v1 whole, which is shorter than its diff:
```python
import functools
import math

import jax
import jax.numpy as jnp
from jax import lax
from jax.experimental import pallas as pl
from jax.experimental.pallas import tpu as pltpu
from jax.sharding import PartitionSpec as P

K = 2


def spectral_tables(nlon, modes):
    longitude = jnp.arange(nlon, dtype=jnp.int32)
    wavenumber = jnp.arange(modes, dtype=jnp.int32)
    product_mod = longitude[:, None] * wavenumber[None, :] % nlon
    phase_angle = product_mod.astype(jnp.float32) * (2.0 * math.pi / nlon)
    wave = jnp.stack([jnp.cos(phase_angle), -jnp.sin(phase_angle)], axis=1)
    weight = jnp.where(wavenumber == 0, 1.0, 2.0).astype(jnp.float32) / nlon
    return wave.astype(jnp.bfloat16), (wave * weight).astype(jnp.bfloat16)


def modes_kernel(field_ref, wave_ref, out_ref, lanes_ref):
    parts, group, width, channels = field_ref.shape
    tall = wave_ref.shape[0]
    half = channels // 2

    def one_row(row, carry):
        column = jnp.concatenate([field_ref[a, row] for a in range(parts)], axis=0)
        spectra = jnp.dot(wave_ref[...], column, preferred_element_type=jnp.float32)
        for h in range(2):
            lanes_ref[h, pl.ds(row, tall, stride=group), :] = spectra[:, h * half : (h + 1) * half]
        return carry

    lax.fori_loop(0, group, one_row, 0)
    slab = 32

    def one_slab(i, carry):
        rows = pl.ds(pl.multiple_of(i * slab * group, slab * group), slab * group)
        for h in range(2):
            piece = lanes_ref[h, rows, :].reshape(slab, group, half)
            out_ref[pl.ds(i * slab, slab), :, h * half : (h + 1) * half] = piece.astype(out_ref.dtype)
        return carry

    lax.fori_loop(0, tall // slab, one_slab, 0)


def grid_kernel(spectra_ref, wave_ref, out_ref, lanes_ref):
    parts, group, width, channels = out_ref.shape
    tall = wave_ref.shape[1]
    half = channels // 2
    slab = 32

    def one_slab(i, carry):
        rows = pl.ds(pl.multiple_of(i * slab * group, slab * group), slab * group)
        for h in range(2):
            piece = spectra_ref[pl.ds(i * slab, slab), :, h * half : (h + 1) * half].astype(jnp.float32)
            lanes_ref[h, rows, :] = piece.reshape(slab * group, half)
        return carry

    lax.fori_loop(0, tall // slab, one_slab, 0)

    def one_row(row, carry):
        column = jnp.concatenate(
            [lanes_ref[h, pl.ds(row, tall, stride=group), :].astype(jnp.bfloat16) for h in range(2)], axis=1
        )
        field = jnp.dot(wave_ref[...], column, preferred_element_type=jnp.float32)
        for a in range(parts):
            out_ref[a, row] = field[a * width : (a + 1) * width].astype(out_ref.dtype)
        return carry

    lax.fori_loop(0, group, one_row, 0)


def transform(kernel, field, wave, shape):
    tall, group, channels = field.shape if len(field.shape) == 3 else shape
    return pl.pallas_call(
        kernel,
        out_shape=jax.ShapeDtypeStruct(shape, field.dtype),
        in_specs=[pl.BlockSpec(memory_space=pltpu.VMEM)] * 2,
        out_specs=pl.BlockSpec(memory_space=pltpu.VMEM),
        scratch_shapes=[pltpu.VMEM((2, tall * group, channels // 2), jnp.float32)],
        compiler_params=pltpu.CompilerParams(vmem_limit_bytes=40 * 2**20),
        cost_estimate=pl.CostEstimate(
            flops=2 * wave.size * group * channels, bytes_accessed=4 * field.size, transcendentals=0
        ),
    )(field, wave)


def couple_kernel(own_ref, low_ref, high_ref, weave_ref, gains_ref, mix_ref, out_ref):
    parts, step, _, group, channels = own_ref.shape
    span = 2 * parts * group

    def whole_column(ref, mode):
        if group % 16 == 0:
            return jnp.concatenate([ref[a, mode, p] for p in range(2) for a in range(parts)], axis=0)
        pieces = [ref[a, mode, p].astype(jnp.float32) for p in range(2) for a in range(parts)]
        return jnp.concatenate(pieces, axis=0).astype(jnp.bfloat16)

    def one_mode(mode, carry):
        sources = [whole_column(ref, mode) for ref in (low_ref, own_ref, high_ref)]
        source = jnp.concatenate(sources, axis=0)
        gains = gains_ref[mode]
        total = jnp.zeros((span, channels), jnp.float32)
        for k in range(K):
            matrix = jnp.concatenate(
                [(weave_ref[k] * gains[2 * k + p][None, :]).astype(jnp.bfloat16) for p in range(2)], axis=0
            )
            summed = jnp.dot(matrix, source, preferred_element_type=jnp.float32)
            total += jnp.dot(summed.astype(jnp.bfloat16), mix_ref[k], preferred_element_type=jnp.float32)
        for p in range(2):
            for a in range(parts):
                first = (p * parts + a) * group
                out_ref[a, mode, p] = total[first : first + group].astype(out_ref.dtype)
        return carry

    lax.fori_loop(0, step, one_mode, 0, unroll=4)


def couple(own, low, high, weave, gains, mix):
    parts, modes, _, group, channels = own.shape
    span = 2 * parts * group
    step = 8
    field = pl.BlockSpec((parts, step, 2, group, channels), lambda i: (0, i, 0, 0, 0))
    return pl.pallas_call(
        couple_kernel,
        grid=(modes // step,),
        out_shape=jax.ShapeDtypeStruct(own.shape, own.dtype),
        in_specs=[
            field,
            field,
            field,
            pl.BlockSpec(weave.shape, lambda i: (0, 0, 0)),
            pl.BlockSpec((step,) + gains.shape[1:], lambda i: (i, 0, 0)),
            pl.BlockSpec(mix.shape, lambda i: (0, 0, 0)),
        ],
        out_specs=field,
        compiler_params=pltpu.CompilerParams(vmem_limit_bytes=24 * 2**20),
        cost_estimate=pl.CostEstimate(
            flops=modes * 2 * channels * span * K * (3 * span + channels),
            bytes_accessed=4 * own.size * 2,
            transcendentals=0,
        ),
    )(own, low, high, weave, gains, mix)


def dense_slots(coupling, filters, counts, offsets, basis):
    slots = coupling.shape[1]
    used = jnp.arange(slots, dtype=jnp.int32)[None] < counts[:, None]
    pairs = jnp.arange(3 * K, dtype=jnp.int32)
    hot = used[:, :, None] & (((offsets + 1) * K + basis)[:, :, None] == pairs)
    mats = jnp.zeros((coupling.shape[0], 3 * K) + coupling.shape[2:], jnp.float32)
    gains = jnp.zeros((coupling.shape[0], 3 * K) + filters.shape[2:], jnp.float32)
    for s in range(slots):
        pick = hot[:, s, :, None, None]
        mats += jnp.where(pick, coupling[:, s, None].astype(jnp.float32), 0.0)
        gains += jnp.where(pick, filters[:, s, None], 0.0)
    return (
        mats.reshape((-1, 3, K) + mats.shape[2:]),
        gains.reshape((-1, 3, K) + gains.shape[2:]),
    )


def weave_of(mats, gains):
    rows = mats.shape[2]
    weave = jnp.stack([mats, mats], axis=3)
    weave = jnp.transpose(weave, (1, 2, 0, 3, 4)).reshape(K, rows, 6 * rows)
    real, imag = gains[:, :, 0], gains[:, :, 1]
    table = jnp.stack([jnp.stack([real, -imag], 0), jnp.stack([imag, real], 0)], 0)
    table = jnp.transpose(table, (4, 3, 0, 2, 1))
    modes = table.shape[0]
    table = jnp.broadcast_to(table[..., None], table.shape + (rows,))
    return weave, table.reshape(modes, 2 * K, 6 * rows)


def per_device(signal, cotangent, mixing, coupling, filters, band_counts, band_offsets, band_basis):
    parts = lax.axis_size("azimuth")
    blocks = lax.axis_size("polar")
    me = lax.axis_index("polar")
    rows, width, channels = signal.shape
    group = rows // parts
    mode_local = filters.shape[3]
    modes = mode_local * parts
    forward, inverse = spectral_tables(width * parts, modes)

    swap = functools.partial(lax.all_to_all, axis_name="azimuth", split_axis=0, concat_axis=0)

    mats, gains = dense_slots(coupling, filters, band_counts, band_offsets, band_basis)
    weave, table = weave_of(mats[me], gains[me])
    near = [jnp.clip(me + step, 0, blocks - 1) for step in (-1, 0, 1)]
    inside = [(me + step >= 0) & (me + step < blocks) for step in (-1, 0, 1)]
    back_mats = jnp.stack([jnp.swapaxes(mats[near[i], 2 - i], 1, 2) for i in range(3)])
    back_gains = jnp.stack([jnp.where(inside[i], gains[near[i], 2 - i], 0.0) for i in range(3)])
    back_gains = back_gains * jnp.array([1.0, -1.0], jnp.float32)[:, None]
    back_weave, back_table = weave_of(back_mats, back_gains)

    tall = 2 * modes

    def by_wave(wave):
        return jnp.swapaxes(wave, 1, 2).reshape(parts * width, tall)

    def to_modes(field, wave):
        spread = swap(field.reshape(parts, group, width, channels))
        spectra = transform(modes_kernel, spread, jnp.transpose(by_wave(wave)), (tall, group, channels))
        return swap(spectra.reshape(parts, mode_local, 2, group, channels))

    def halo(own):
        low = lax.ppermute(own, "polar", [(i, i + 1) for i in range(blocks - 1)])
        high = lax.ppermute(own, "polar", [(i + 1, i) for i in range(blocks - 1)])
        return low, high

    def to_grid(spectra, wave):
        spectra = swap(spectra).reshape(tall, group, channels)
        field = transform(grid_kernel, spectra, by_wave(wave), (parts, group, width, channels))
        return swap(field).reshape(rows, width, channels)

    first = to_modes(signal, forward)
    second = to_modes(cotangent, inverse)
    first_halo = halo(first)
    second_halo = halo(second)
    out_spectra = couple(first, *first_halo, weave, table, mixing)
    grad_spectra = couple(
        second, *second_halo, back_weave, back_table, jnp.swapaxes(mixing, 1, 2)
    )
    return to_grid(out_spectra, inverse), to_grid(grad_spectra, forward)


def solution(mesh):
    return jax.shard_map(
        per_device,
        mesh=mesh,
        in_specs=(
            P("polar", "azimuth", None),
            P("polar", "azimuth", None),
            P(),
            P(),
            P(None, None, None, "azimuth"),
            P(),
            P(),
            P(),
        ),
        out_specs=(P("polar", "azimuth", None), P("polar", "azimuth", None)),
        check_vma=False,
    )
```

time: 1820 us -> 662 us (0.36)
  local copies, waits for them, and re-layouts: 726 us -> 55 us
  blocking collectives: 378 us -> 77.1 us
  other arithmetic: 257 us -> 8.81 us
  Pallas kernels: 0 us -> 116 us
  waiting for transfers between devices: 244 us -> 349 us
  loops' own time: 92.9 us -> 0 us
  matrix products: 91.3 us -> 0 us
  starting transfers between devices: 21.9 us -> 51.9 us
    all_to_all x3 -> x1, blocking collectives: 378 us -> 77.1 us  [to_modes(): spread = swap(field.reshape(parts, group, width, channels))]
    all_to_all x9 -> x0, local copies, waits for them, and re-layouts: 201 us -> none  [the longest x2 62.4 us: per_device(): lax.all_to_all(stacked, 'azimuth', split_axis=4, concat_axis=0, tiled=True)]
    all_to_all x2 -> x7, waiting for transfers between devices: 133 us -> 328 us  [the longest x2 119 us: to_grid(): return swap(field).reshape(rows, width, channels)]
    unnamed x44 -> x33, local copies, waits for them, and re-layouts: 194 us -> 32.5 us
    add x11 -> x3, other arithmetic: 122 us -> 2.19 us  [the longest x1 1.7 us: dense_slots(): mats += jnp.where(pick, coupling[:, s, None].astype(jnp.float32), 0.0)]
    pallas_call x0 -> x6, Pallas kernels: none -> 116 us  [the longest x4 59.5 us: transform(): pl.pallas_call(kernel, out_shape=jax.ShapeDtypeStruct(shape, field.dtype)...]
    another operation x56 -> x0, loops' own time: 92.9 us -> none  [the longest x6 71.2 us: backward_basis(): running = lax.fori_loop(0, slot_count, backward_slot, running)]
    another operation x3, local copies, waits for them, and re-layouts: 94.3 us -> 1.98 us  [the longest x2 1.04 us: per_device(): jnp.stack([jnp.swapaxes(mats[near[i], 2 - i], 1, 2) for i in range(3)])]
  transfers between devices with their start and end apart: 4 -> 11, of which waited for: 3 -> 9; matrix products, arithmetic and copies ran while one was open for 8% -> 5% of each run, Pallas kernels for 0% -> 18%
where the time goes in v1:
time: 662 us; the launch traced here: 659 us
  waiting for transfers between devices  349 us (53%)
  Pallas kernels  116 us (18%)
  blocking collectives  77.1 us (12%)
  local copies, waits for them, and re-layouts  55 us (8%)
  starting transfers between devices  51.9 us (8%)
  other arithmetic  8.81 us (1%)
    all_to_all x2, waiting for transfers between devices, to_grid(): return swap(field).reshape(rows, width, channels)  119 us
    all_to_all x2, waiting for transfers between devices, to_modes(): return swap(spectra.reshape(parts, mode_local, 2, group, channels))  105 us
    all_to_all x1, blocking collectives, to_modes(): spread = swap(field.reshape(parts, group, width, channels))  77.1 us
    all_to_all x2, waiting for transfers between devices, to_grid(): spectra = swap(spectra).reshape(tall, group, channels)  62.7 us
    pallas_call x4, Pallas kernels, transform(): pl.pallas_call(kernel, out_shape=jax.ShapeDtypeStruct(shape, field.dtype)...  59.5 us
    pallas_call x2, Pallas kernels, couple(): pl.pallas_call(couple_kernel, grid=(modes // step,), out_shape=jax.ShapeD...  56.7 us
    all_to_all x1, waiting for transfers between devices, to_modes(): spread = swap(field.reshape(parts, group, width, channels))  40.5 us
    unnamed x33, local copies, waits for them, and re-layouts  32.5 us
  transfers between devices with their start and end apart: 11, of which 9 were waited for; matrix products, arithmetic and copies ran while one was open for 5% of the time, Pallas kernels for 18%

profile of v1, /device:TPU:1, one launch (start us, length us, event | category | flops | bytes accessed | tf_op | source)
XLA Modules:
  0.0 658.8 jit_solution(13347880856077954887)
XLA Ops:
  0.6 77.1 %all_to_all.40.field_ref = bf16[4,16,192,256]{3,2,1,0:T(8,128)(2,1)} all-to-all(bf16[4,16,192,256]{3,2,1,0:T(8,128)(2,1)} %bitcast.117), channel_id=1, replica_groups=mesh['polar'=8,'azimuth'=4] {'azimuth'}, dimensions={0} | all-to-all | bytes 12582912 | tf_op jit(solution)/shard_map/all_to_all | solution.py:204
  77.7 5.3 all-to-all-start
  83.0 4.8 sine_negate_fusion
  88.0 2.8 copy.101
  90.8 3.0 reshape.230
  93.8 2.8 copy-done.4
  96.6 12.4 %shard_map.107 = bf16[768,16,256]{2,1,0:T(8,128)(2,1)S(1)} custom-call(bf16[4,16,192,256]{3,2,1,0:T(8,128)(2,1)S(1)} %copy-done.4, bf16[768,768]{1,0:T(8,128)(2,1)S(1)} %bitcast.114), custom_call_target="tpu_custom_call" | custom-call | flops 4831838208 | bytes 12582912 | tf_op jit(solution)/shard_map/pallas_call | solution.py:78
  109.0 2.7 copy-done.3
  111.7 40.5 %all-to-all-done.field_ref = bf16[4,16,192,256]{3,2,1,0:T(8,128)(2,1)} async-done(((bf16[4,16,192,256]{3,2,1,0:T(8,128)(2,1)}), bf16[4,16,192,256]{3,2,1,0:T(8,128)(2,1)}, u32[]{:S(2)}, u32[]{:S(2)}) %all-to-all-start) | async-done | bytes 6291488 | tf_op jit(solution)/shard_map/all_to_all | solution.py:204
  152.3 5.3 all-to-all-start.5
  157.5 1.2 fusion.3
  158.7 3.6 copy.84
  162.9 15.2 %shard_map.104 = bf16[768,16,256]{2,1,0:T(8,128)(2,1)S(1)} custom-call(bf16[4,16,192,256]{3,2,1,0:T(8,128)(2,1)} %all-to-all-done.field_ref, bf16[768,768]{1,0:T(8,128)(2,1)S(1)} %bitcast.115), custom_call_target="tpu_custom_call" | custom-call | flops 4831838208 | bytes 12582912 | tf_op jit(solution)/shard_map/pallas_call | solution.py:78
  178.1 2.7 copy-done
  180.8 46.0 %all-to-all-done.5.own_ref = bf16[4,96,2,16,256]{4,3,2,1,0:T(8,128)(2,1)} async-done(((bf16[4,96,2,16,256]{4,3,2,1,0:T(8,128)(2,1)}), bf16[4,96,2,16,256]{4,3,2,1,0:T(8,128)(2,1)}, u32[]{:S(2)}, u32[]{:S(2)}) %all-to-all-start.5) | async-done | bytes 6291488 | tf_op jit(solution)/shard_map/all_to_all | solution.py:206
  226.9 5.4 all-to-all-start.1
  232.3 4.3 collective-permute-start.2
  236.6 3.1 collective-permute-start.3
  240.9 1.7 select_add_fusion
  242.6 59.0 %all-to-all-done.1.own_ref = bf16[4,96,2,16,256]{4,3,2,1,0:T(8,128)(2,1)} async-done(((bf16[4,96,2,16,256]{4,3,2,1,0:T(8,128)(2,1)}), bf16[4,96,2,16,256]{4,3,2,1,0:T(8,128)(2,1)}, u32[]{:S(2)}, u32[]{:S(2)}) %all-to-all-start.1) | async-done | bytes 6291488 | tf_op jit(solution)/shard_map/all_to_all | solution.py:206
  301.6 4.3 collective-permute-start
  305.9 3.2 collective-permute-start.1
  310.6 1.0 reshape.234.weave_ref
  313.2 1.4 copy.107.gains_ref
  315.7 28.2 %shard_map.108 = bf16[4,96,2,16,256]{4,3,2,1,0:T(8,128)(2,1)S(1)} custom-call(bf16[4,96,2,16,256]{4,3,2,1,0:T(8,128)(2,1)} %all-to-all-done.5.own_ref, bf16[4,96,2,16,256]{4,3,2,1,0:T(8,128)(2,1)} %collective-permute-done.2.low_ref, bf16[4,96,2,16,256]{4,3,2,1,0:T(8,128)(2,1)} %collective-permute-done.3.high_ref, f32[2,64,384]{2,1,0:T(8,128)S(1)} %copy-done.8, ...), custom_call_target="tpu_custom_call" | custom-call | flops 8053063680 | bytes 25165824 | tf_op jit(solution)/shard_map/pallas_call | solution.py:126
  343.9 2.7 copy-done.1
  346.6 5.3 all-to-all-start.6
  352.9 1.4 copy.100.gains_ref
  354.4 0.9 dynamic-slice_bitcast_fusion
  355.4 1.1 copy.92
  356.4 1.3 reshape.227.weave_ref
  357.7 16.4 %collective-permute-done.low_ref = bf16[4,96,2,16,256]{4,3,2,1,0:T(8,128)(2,1)} collective-permute-done((bf16[4,96,2,16,256]{4,3,2,1,0:T(8,128)(2,1)}, bf16[4,96,2,16,256]{4,3,2,1,0:T(8,128)(2,1)}, u32[]{:S(2)}, u32[]{:S(2)}) %collective-permute-start) | collective-permute-done | bytes 6291488 | tf_op jit(solution)/shard_map/ppermute | solution.py:209
  374.1 4.7 collective-permute-done.1.high_ref
  378.8 28.4 %shard_map.105 = bf16[4,96,2,16,256]{4,3,2,1,0:T(8,128)(2,1)S(1)} custom-call(bf16[4,96,2,16,256]{4,3,2,1,0:T(8,128)(2,1)} %all-to-all-done.1.own_ref, bf16[4,96,2,16,256]{4,3,2,1,0:T(8,128)(2,1)} %collective-permute-done.low_ref, bf16[4,96,2,16,256]{4,3,2,1,0:T(8,128)(2,1)} %collective-permute-done.1.high_ref, f32[2,64,384]{2,1,0:T(8,128)S(1)} %reshape.227.weave_ref, ...), custom_call_target="tpu_custom_call" | custom-call | flops 8053063680 | bytes 25165824 | tf_op jit(solution)/shard_map/pallas_call | solution.py:126
  407.2 2.7 copy-done.2
  409.9 12.4 %all-to-all-done.6 = bf16[4,96,2,16,256]{4,3,2,1,0:T(8,128)(2,1)} async-done(((bf16[4,96,2,16,256]{4,3,2,1,0:T(8,128)(2,1)}), bf16[4,96,2,16,256]{4,3,2,1,0:T(8,128)(2,1)}, u32[]{:S(2)}, u32[]{:S(2)}) %all-to-all-start.6) | async-done | bytes 6291488 | tf_op jit(solution)/shard_map/all_to_all | solution.py:214
  422.3 5.2 all-to-all-start.2
  428.2 15.9 %shard_map.109 = bf16[4,16,192,256]{3,2,1,0:T(8,128)(2,1)S(1)} custom-call(bf16[768,16,256]{2,1,0:T(8,128)(2,1)} %bitcast.52.spectra_ref, bf16[768,768]{1,0:T(8,128)(2,1)S(1)} %copy.108.wave_ref), custom_call_target="tpu_custom_call" | custom-call | flops 4831838208 | bytes 12582912 | tf_op jit(solution)/shard_map/pallas_call | solution.py:78
  444.2 2.7 copy-done.5
  446.9 50.3 %all-to-all-done.2 = bf16[4,96,2,16,256]{4,3,2,1,0:T(8,128)(2,1)} async-done(((bf16[4,96,2,16,256]{4,3,2,1,0:T(8,128)(2,1)}), bf16[4,96,2,16,256]{4,3,2,1,0:T(8,128)(2,1)}, u32[]{:S(2)}, u32[]{:S(2)}) %all-to-all-start.2) | async-done | bytes 6291488 | tf_op jit(solution)/shard_map/all_to_all | solution.py:214
  497.2 5.3 all-to-all-start.7
  503.1 15.9 %shard_map.106 = bf16[4,16,192,256]{3,2,1,0:T(8,128)(2,1)S(1)} custom-call(bf16[768,16,256]{2,1,0:T(8,128)(2,1)} %bitcast.25.spectra_ref, bf16[768,768]{1,0:T(8,128)(2,1)S(1)} %copy.102.wave_ref), custom_call_target="tpu_custom_call" | custom-call | flops 4831838208 | bytes 12582912 | tf_op jit(solution)/shard_map/pallas_call | solution.py:78
  519.0 2.7 copy-done.6
  521.7 50.1 %all-to-all-done.7 = bf16[4,16,192,256]{3,2,1,0:T(8,128)(2,1)} async-done(((bf16[4,16,192,256]{3,2,1,0:T(8,128)(2,1)}), bf16[4,16,192,256]{3,2,1,0:T(8,128)(2,1)}, u32[]{:S(2)}, u32[]{:S(2)}) %all-to-all-start.7) | async-done | bytes 6291488 | tf_op jit(solution)/shard_map/all_to_all | solution.py:216
  571.8 5.3 all-to-all-start.3
  577.0 69.3 %all-to-all-done.3 = bf16[4,16,192,256]{3,2,1,0:T(8,128)(2,1)} async-done(((bf16[4,16,192,256]{3,2,1,0:T(8,128)(2,1)}), bf16[4,16,192,256]{3,2,1,0:T(8,128)(2,1)}, u32[]{:S(2)}, u32[]{:S(2)}) %all-to-all-start.3) | async-done | bytes 6291488 | tf_op jit(solution)/shard_map/all_to_all | solution.py:216
  646.3 6.2 copy.111
  652.6 6.2 copy.112
  (72 shorter events, 8.2 us)
Async XLA Ops:
  77.7 74.6 %all-to-all-start = ((bf16[4,16,192,256]{3,2,1,0:T(8,128)(2,1)}), bf16[4,16,192,256]{3,2,1,0:T(8,128)(2,1)}, u32[]{:S(2)}, u32[]{:S(2)}) async-start(bf16[4,16,192,256]{3,2,1,0:T(8,128)(2,1)} %bitcast.118), calls=%async_computation | async-start | bytes 12582912 | tf_op jit(solution)/shard_map/all_to_all | solution.py:204
  93.8 2.8 copy-start.4
  109.0 2.7 copy-start.3
  152.3 74.6 %all-to-all-start.5 = ((bf16[4,96,2,16,256]{4,3,2,1,0:T(8,128)(2,1)}), bf16[4,96,2,16,256]{4,3,2,1,0:T(8,128)(2,1)}, u32[]{:S(2)}, u32[]{:S(2)}) async-start(bf16[4,96,2,16,256]{4,3,2,1,0:T(8,128)(2,1)} %bitcast.113), calls=%async_computation.5 | async-start | bytes 12582912 | tf_op jit(solution)/shard_map/all_to_all | solution.py:206
  178.1 2.7 copy-start
  226.9 12.9 %copy-start.11 = (s32[8,6]{1,0:T(8,128)S(1)}, s32[8,6]{1,0:T(8,128)}, u32[]{:S(2)}) copy-start(s32[8,6]{1,0:T(8,128)} %param.16) | copy-start | bytes 580
  226.9 12.9 %copy-start.12 = (s32[8,6]{1,0:T(8,128)S(1)}, s32[8,6]{1,0:T(8,128)}, u32[]{:S(2)}) copy-start(s32[8,6]{1,0:T(8,128)} %param.15) | copy-start | bytes 580
  226.9 13.0 %copy-start.14 = (s32[8]{0:T(128)S(1)}, s32[8]{0:T(128)}, u32[]{:S(2)}) copy-start(s32[8]{0:T(128)} %param.14) | copy-start | bytes 100
  226.9 13.8 %copy-start.9 = (bf16[8,6,64,64]{3,2,1,0:T(8,128)(2,1)S(1)}, bf16[8,6,64,64]{3,2,1,0:T(8,128)(2,1)}, u32[]{:S(2)}) copy-start(bf16[8,6,64,64]{3,2,1,0:T(8,128)(2,1)} %param.12) | copy-start | bytes 1179652
  226.9 74.7 %all-to-all-start.1 = ((bf16[4,96,2,16,256]{4,3,2,1,0:T(8,128)(2,1)}), bf16[4,96,2,16,256]{4,3,2,1,0:T(8,128)(2,1)}, u32[]{:S(2)}, u32[]{:S(2)}) async-start(bf16[4,96,2,16,256]{4,3,2,1,0:T(8,128)(2,1)} %bitcast.112), calls=%async_computation.1 | async-start | bytes 12582912 | tf_op jit(solution)/shard_map/all_to_all | solution.py:206
  232.3 82.5 %collective-permute-start.2 = (bf16[4,96,2,16,256]{4,3,2,1,0:T(8,128)(2,1)}, bf16[4,96,2,16,256]{4,3,2,1,0:T(8,128)(2,1)}, u32[]{:S(2)}, u32[]{:S(2)}) collective-permute-start(bf16[4,96,2,16,256]{4,3,2,1,0:T(8,128)(2,1)} %all-to-all-done.5.own_ref), channel_id=1, source_target_pairs={{0,4},{4,8},{8,12},{12,16},{16,20},{20,24},{24,28},{1,5},{5,9},{9,... | collective-permute-start | bytes 18874376 | tf_op jit(solution)/shard_map/ppermute | solution.py:209
  236.6 78.2 %collective-permute-start.3 = (bf16[4,96,2,16,256]{4,3,2,1,0:T(8,128)(2,1)}, bf16[4,96,2,16,256]{4,3,2,1,0:T(8,128)(2,1)}, u32[]{:S(2)}, u32[]{:S(2)}) collective-permute-start(bf16[4,96,2,16,256]{4,3,2,1,0:T(8,128)(2,1)} %all-to-all-done.5.own_ref), channel_id=1, source_target_pairs={{4,0},{8,4},{12,8},{16,12},{20,16},{24,20},{28,24},{5,1},{9,5},{13... | collective-permute-start | bytes 18874376 | tf_op jit(solution)/shard_map/ppermute | solution.py:210
  242.6 69.0 %copy-start.10 = (f32[8,6,2,96]{3,2,1,0:T(2,128)S(1)}, f32[8,6,2,96]{3,2,1,0:T(2,128)}, u32[]{:S(2)}) copy-start(f32[8,6,2,96]{3,2,1,0:T(2,128)} %param.13) | copy-start | bytes 110596
  301.6 72.5 %collective-permute-start = (bf16[4,96,2,16,256]{4,3,2,1,0:T(8,128)(2,1)}, bf16[4,96,2,16,256]{4,3,2,1,0:T(8,128)(2,1)}, u32[]{:S(2)}, u32[]{:S(2)}) collective-permute-start(bf16[4,96,2,16,256]{4,3,2,1,0:T(8,128)(2,1)} %all-to-all-done.1.own_ref), channel_id=1, source_target_pairs={{0,4},{4,8},{8,12},{12,16},{16,20},{20,24},{24,28},{1,5},{5,9},{9,... | collective-permute-start | bytes 18874376 | tf_op jit(solution)/shard_map/ppermute | solution.py:209
  305.9 72.9 %collective-permute-start.1 = (bf16[4,96,2,16,256]{4,3,2,1,0:T(8,128)(2,1)}, bf16[4,96,2,16,256]{4,3,2,1,0:T(8,128)(2,1)}, u32[]{:S(2)}, u32[]{:S(2)}) collective-permute-start(bf16[4,96,2,16,256]{4,3,2,1,0:T(8,128)(2,1)} %all-to-all-done.1.own_ref), channel_id=1, source_target_pairs={{4,0},{8,4},{12,8},{16,12},{20,16},{24,20},{28,24},{5,1},{9,5},{13... | collective-permute-start | bytes 18874376 | tf_op jit(solution)/shard_map/ppermute | solution.py:210
  310.0 2.1 copy-start.13
  310.5 4.1 copy-start.7
  314.8 0.9 copy-start.8
  343.9 2.7 copy-start.1
  346.6 75.7 %all-to-all-start.6 = ((bf16[4,96,2,16,256]{4,3,2,1,0:T(8,128)(2,1)}), bf16[4,96,2,16,256]{4,3,2,1,0:T(8,128)(2,1)}, u32[]{:S(2)}, u32[]{:S(2)}) async-start(bf16[4,96,2,16,256]{4,3,2,1,0:T(8,128)(2,1)} %copy-done.1), calls=%async_computation.6 | async-start | bytes 12582912 | tf_op jit(solution)/shard_map/all_to_all | solution.py:214
  407.2 2.7 copy-start.2
  422.3 74.8 %all-to-all-start.2 = ((bf16[4,96,2,16,256]{4,3,2,1,0:T(8,128)(2,1)}), bf16[4,96,2,16,256]{4,3,2,1,0:T(8,128)(2,1)}, u32[]{:S(2)}, u32[]{:S(2)}) async-start(bf16[4,96,2,16,256]{4,3,2,1,0:T(8,128)(2,1)} %copy-done.2), calls=%async_computation.2 | async-start | bytes 12582912 | tf_op jit(solution)/shard_map/all_to_all | solution.py:214
  444.1 2.7 copy-start.5
  497.2 74.6 %all-to-all-start.7 = ((bf16[4,16,192,256]{3,2,1,0:T(8,128)(2,1)}), bf16[4,16,192,256]{3,2,1,0:T(8,128)(2,1)}, u32[]{:S(2)}, u32[]{:S(2)}) async-start(bf16[4,16,192,256]{3,2,1,0:T(8,128)(2,1)} %copy-done.5), calls=%async_computation.7 | async-start | bytes 12582912 | tf_op jit(solution)/shard_map/all_to_all | solution.py:216
  519.0 2.7 copy-start.6
  571.8 74.6 %all-to-all-start.3 = ((bf16[4,16,192,256]{3,2,1,0:T(8,128)(2,1)}), bf16[4,16,192,256]{3,2,1,0:T(8,128)(2,1)}, u32[]{:S(2)}, u32[]{:S(2)}) async-start(bf16[4,16,192,256]{3,2,1,0:T(8,128)(2,1)} %copy-done.6), calls=%async_computation.3 | async-start | bytes 12582912 | tf_op jit(solution)/shard_map/all_to_all | solution.py:216

commit v2 on v1

v2 whole, which is shorter than its diff:
```python
import functools
import math

import jax
import jax.numpy as jnp
from jax import lax
from jax.experimental import pallas as pl
from jax.experimental.pallas import tpu as pltpu
from jax.sharding import PartitionSpec as P

K = 2
LANES = 128


def spectral_tables(nlon, modes):
    longitude = jnp.arange(nlon, dtype=jnp.int32)
    wavenumber = jnp.arange(modes, dtype=jnp.int32)
    product_mod = longitude[:, None] * wavenumber[None, :] % nlon
    phase_angle = product_mod.astype(jnp.float32) * (2.0 * math.pi / nlon)
    wave = jnp.stack([jnp.cos(phase_angle), -jnp.sin(phase_angle)], axis=1)
    weight = jnp.where(wavenumber == 0, 1.0, 2.0).astype(jnp.float32) / nlon
    return wave.astype(jnp.bfloat16), (wave * weight).astype(jnp.bfloat16)


def pack_kernel(field_ref, pick_ref, out_ref):
    fold = field_ref.shape[0]
    parts, _, _, lanes = out_ref.shape
    wide = jnp.concatenate([field_ref[h, 0] for h in range(fold)], axis=1)
    packed = jnp.dot(wide, pick_ref[...], preferred_element_type=jnp.float32)
    for g in range(parts):
        out_ref[g, 0] = packed[:, g * lanes : (g + 1) * lanes].astype(out_ref.dtype)


def pack(field, pick, parts, fold):
    rows, width, channels = field.shape
    slim = rows // fold
    return pl.pallas_call(
        pack_kernel,
        grid=(slim,),
        out_shape=jax.ShapeDtypeStruct((parts, slim, width, LANES), field.dtype),
        in_specs=[
            pl.BlockSpec((fold, 1, width, channels), lambda i: (0, i, 0, 0)),
            pl.BlockSpec(pick.shape, lambda i: (0, 0)),
        ],
        out_specs=pl.BlockSpec((parts, 1, width, LANES), lambda i: (0, i, 0, 0)),
        compiler_params=pltpu.CompilerParams(vmem_limit_bytes=16 * 2**20),
        cost_estimate=pl.CostEstimate(
            flops=2 * field.size * parts * LANES, bytes_accessed=4 * field.size, transcendentals=0
        ),
    )(field.reshape(fold, slim, width, channels), pick)


def mix_kernel(*refs):
    mix_ref, out_ref = refs[K:]
    fold, _, _, channels = out_ref.shape
    wide = jnp.concatenate([ref[g, 0] for ref in refs[:K] for g in range(refs[0].shape[0])], axis=1)
    mixed = jnp.dot(wide, mix_ref[...], preferred_element_type=jnp.float32)
    for h in range(fold):
        out_ref[h, 0] = mixed[:, h * channels : (h + 1) * channels].astype(out_ref.dtype)


def mix_last(fields, mix, fold):
    parts, slim, width, lanes = fields[0].shape
    channels = mix.shape[1] // fold
    out = pl.pallas_call(
        mix_kernel,
        grid=(slim,),
        out_shape=jax.ShapeDtypeStruct((fold, slim, width, channels), fields[0].dtype),
        in_specs=[pl.BlockSpec((parts, 1, width, lanes), lambda i: (0, i, 0, 0))] * K
        + [pl.BlockSpec(mix.shape, lambda i: (0, 0))],
        out_specs=pl.BlockSpec((fold, 1, width, channels), lambda i: (0, i, 0, 0)),
        compiler_params=pltpu.CompilerParams(vmem_limit_bytes=16 * 2**20),
        cost_estimate=pl.CostEstimate(
            flops=2 * slim * width * mix.size, bytes_accessed=6 * fields[0].size, transcendentals=0
        ),
    )(*fields, mix)
    return out.reshape(fold * slim, width, channels)


def modes_kernel(field_ref, wave_ref, out_ref, lanes_ref):
    parts, slim, width, lanes = field_ref.shape
    tall = wave_ref.shape[0]
    half = slim // 2

    def one_pair(row, carry):
        column = jnp.concatenate(
            [
                jnp.concatenate([field_ref[a, row + h * half] for a in range(parts)], axis=0)
                for h in range(2)
            ],
            axis=1,
        )
        spectra = jnp.dot(wave_ref[...], column, preferred_element_type=jnp.float32)
        for h in range(2):
            lanes_ref[pl.ds(row + h * half, tall, stride=slim), :] = spectra[:, h * lanes : (h + 1) * lanes]
        return carry

    lax.fori_loop(0, half, one_pair, 0)
    slab = 32

    def one_slab(i, carry):
        rows = pl.ds(pl.multiple_of(i * slab * slim, slab * slim), slab * slim)
        piece = lanes_ref[rows, :].reshape(slab, slim, lanes)
        out_ref[pl.ds(i * slab, slab)] = piece.astype(out_ref.dtype)
        return carry

    lax.fori_loop(0, tall // slab, one_slab, 0)


def grid_kernel(spectra_ref, wave_ref, out_ref, lanes_ref):
    parts, slim, width, lanes = out_ref.shape
    tall = wave_ref.shape[1]
    half = slim // 2
    slab = 32

    def one_slab(i, carry):
        rows = pl.ds(pl.multiple_of(i * slab * slim, slab * slim), slab * slim)
        lanes_ref[rows, :] = spectra_ref[pl.ds(i * slab, slab)].astype(jnp.float32).reshape(slab * slim, lanes)
        return carry

    lax.fori_loop(0, tall // slab, one_slab, 0)

    def one_pair(row, carry):
        column = jnp.concatenate(
            [
                lanes_ref[pl.ds(row + h * half, tall, stride=slim), :].astype(jnp.bfloat16)
                for h in range(2)
            ],
            axis=1,
        )
        field = jnp.dot(wave_ref[...], column, preferred_element_type=jnp.float32)
        for h in range(2):
            for a in range(parts):
                piece = field[a * width : (a + 1) * width, h * lanes : (h + 1) * lanes]
                out_ref[a, row + h * half] = piece.astype(out_ref.dtype)
        return carry

    lax.fori_loop(0, half, one_pair, 0)


def transform(kernel, field, wave, shape):
    tall, slim, lanes = field.shape if len(field.shape) == 3 else shape
    return pl.pallas_call(
        kernel,
        out_shape=jax.ShapeDtypeStruct(shape, field.dtype),
        in_specs=[pl.BlockSpec(memory_space=pltpu.VMEM)] * 2,
        out_specs=pl.BlockSpec(memory_space=pltpu.VMEM),
        scratch_shapes=[pltpu.VMEM((tall * slim, lanes), jnp.float32)],
        compiler_params=pltpu.CompilerParams(vmem_limit_bytes=40 * 2**20),
        cost_estimate=pl.CostEstimate(
            flops=2 * wave.size * slim * lanes, bytes_accessed=4 * field.size, transcendentals=0
        ),
    )(field, wave)


def couple_kernel(own_ref, low_ref, high_ref, weave_ref, gains_ref, *out_refs):
    step, span, lanes = own_ref.shape
    fold, _, rows, _ = weave_ref.shape
    slim = rows // fold
    part = lanes // fold
    owner = lax.broadcasted_iota(jnp.int32, (slim, lanes), 1) // part

    def one_mode(mode, carry):
        source = jnp.concatenate([ref[mode] for ref in (low_ref, own_ref, high_ref)], axis=0)
        gains = gains_ref[mode]
        matrix = jnp.concatenate(
            [
                (weave_ref[h, k] * gains[2 * k + p][None, :]).astype(jnp.bfloat16)
                for h in range(fold)
                for k in range(K)
                for p in range(2)
            ],
            axis=0,
        )
        spread = jnp.dot(matrix, source, preferred_element_type=jnp.float32)

        def rows_from(h, k, p, to):
            first = (((h * K + k) * 2 + p) * fold + to) * slim
            return spread[first : first + slim]

        for k in range(K):
            for p in range(2):
                total = None
                for turn in range(fold):
                    term = rows_from(0, k, p, (0 - turn) % fold)
                    for h in range(1, fold):
                        term = jnp.where(owner == h, rows_from(h, k, p, (h - turn) % fold), term)
                    if turn:
                        term = pltpu.roll(term, (fold - turn) * part, 1)
                    total = term if total is None else total + term
                out_refs[k][mode, p * slim : (p + 1) * slim] = total.astype(out_refs[k].dtype)
        return carry

    lax.fori_loop(0, step, one_mode, 0, unroll=4)


def couple(own, low, high, weave, gains):
    modes, span, lanes = own.shape
    step = 16
    field = pl.BlockSpec((step, span, lanes), lambda i: (i, 0, 0))
    return pl.pallas_call(
        couple_kernel,
        grid=(modes // step,),
        out_shape=[jax.ShapeDtypeStruct(own.shape, own.dtype)] * K,
        in_specs=[
            field,
            field,
            field,
            pl.BlockSpec(weave.shape, lambda i: (0, 0, 0, 0)),
            pl.BlockSpec((step,) + gains.shape[1:], lambda i: (i, 0, 0)),
        ],
        out_specs=[field] * K,
        compiler_params=pltpu.CompilerParams(vmem_limit_bytes=24 * 2**20),
        cost_estimate=pl.CostEstimate(
            flops=2 * modes * weave.size * 2 * lanes,
            bytes_accessed=10 * own.size,
            transcendentals=0,
        ),
    )(own, low, high, weave, gains)


def dense_slots(coupling, filters, counts, offsets, basis):
    slots = coupling.shape[1]
    used = jnp.arange(slots, dtype=jnp.int32)[None] < counts[:, None]
    pairs = jnp.arange(3 * K, dtype=jnp.int32)
    hot = used[:, :, None] & (((offsets + 1) * K + basis)[:, :, None] == pairs)
    mats = jnp.zeros((coupling.shape[0], 3 * K) + coupling.shape[2:], jnp.float32)
    gains = jnp.zeros((coupling.shape[0], 3 * K) + filters.shape[2:], jnp.float32)
    for s in range(slots):
        pick = hot[:, s, :, None, None]
        mats += jnp.where(pick, coupling[:, s, None].astype(jnp.float32), 0.0)
        gains += jnp.where(pick, filters[:, s, None], 0.0)
    return (
        mats.reshape((-1, 3, K) + mats.shape[2:]),
        gains.reshape((-1, 3, K) + gains.shape[2:]),
    )


def weave_of(mats, gains, fold):
    rows = mats.shape[2]
    slim = rows // fold
    mats = mats.reshape(3, K, rows, fold, slim)
    weave = jnp.stack([mats, mats], axis=4)
    weave = jnp.transpose(weave, (3, 1, 2, 0, 4, 5)).reshape(fold, K, rows, 6 * slim)
    real, imag = gains[:, :, 0], gains[:, :, 1]
    table = jnp.stack([jnp.stack([real, -imag], 0), jnp.stack([imag, real], 0)], 0)
    table = jnp.transpose(table, (4, 3, 0, 2, 1))
    modes = table.shape[0]
    table = jnp.broadcast_to(table[..., None], table.shape + (slim,))
    return weave, table.reshape(modes, 2 * K, 6 * slim)


def per_device(signal, cotangent, mixing, coupling, filters, band_counts, band_offsets, band_basis):
    parts = lax.axis_size("azimuth")
    blocks = lax.axis_size("polar")
    me = lax.axis_index("polar")
    rows, width, channels = signal.shape
    share = channels // parts
    fold = LANES // share
    slim = rows // fold
    filters = lax.all_gather(filters, "azimuth", axis=3, tiled=True)
    modes = filters.shape[3]
    forward, inverse = spectral_tables(width * parts, modes)

    swap = functools.partial(lax.all_to_all, axis_name="azimuth", split_axis=0, concat_axis=0)

    same = jnp.eye(fold, dtype=jnp.bfloat16)
    source = jnp.arange(fold * channels, dtype=jnp.int32)
    target = jnp.arange(parts * LANES, dtype=jnp.int32)
    origin = (target % LANES // share) * channels + target // LANES * share + target % share
    pick = (source[:, None] == origin[None, :]).astype(jnp.bfloat16)

    def widen(mix):
        mix = mix.reshape(K, parts, 1, share, 1, channels) * same.reshape(1, 1, fold, 1, fold, 1)
        return mix.reshape(K * parts * LANES, fold * channels)

    mats, gains = dense_slots(coupling, filters, band_counts, band_offsets, band_basis)
    weave, table = weave_of(mats[me], gains[me], fold)
    near = [jnp.clip(me + step, 0, blocks - 1) for step in (-1, 0, 1)]
    inside = [(me + step >= 0) & (me + step < blocks) for step in (-1, 0, 1)]
    back_mats = jnp.stack([jnp.swapaxes(mats[near[i], 2 - i], 1, 2) for i in range(3)])
    back_gains = jnp.stack([jnp.where(inside[i], gains[near[i], 2 - i], 0.0) for i in range(3)])
    back_gains = back_gains * jnp.array([1.0, -1.0], jnp.float32)[:, None]
    back_weave, back_table = weave_of(back_mats, back_gains, fold)

    tall = 2 * modes

    def by_wave(wave):
        return jnp.swapaxes(wave, 1, 2).reshape(parts * width, tall)

    def to_modes(field, wave):
        spread = swap(pack(field, pick, parts, fold))
        spectra = transform(modes_kernel, spread, jnp.transpose(by_wave(wave)), (tall, slim, LANES))
        return spectra.reshape(modes, 2 * slim, LANES)

    def halo(own):
        low = lax.ppermute(own, "polar", [(i, i + 1) for i in range(blocks - 1)])
        high = lax.ppermute(own, "polar", [(i + 1, i) for i in range(blocks - 1)])
        return low, high

    def to_grid(sums, wave):
        wave = by_wave(wave)
        shape = (parts, slim, width, LANES)
        return [swap(transform(grid_kernel, one.reshape(tall, slim, LANES), wave, shape)) for one in sums]

    first = to_modes(signal, forward)
    second = to_modes(cotangent, inverse)
    first_halo = halo(first)
    second_halo = halo(second)
    sums = couple(first, *first_halo, weave, table)
    back_sums = couple(second, *second_halo, back_weave, back_table)
    output = mix_last(to_grid(sums, inverse), widen(mixing), fold)
    back = to_grid(back_sums, forward)
    return output, mix_last(back, widen(jnp.swapaxes(mixing, 1, 2)), fold)


def solution(mesh):
    return jax.shard_map(
        per_device,
        mesh=mesh,
        in_specs=(
            P("polar", "azimuth", None),
            P("polar", "azimuth", None),
            P(),
            P(),
            P(None, None, None, "azimuth"),
            P(),
            P(),
            P(),
        ),
        out_specs=(P("polar", "azimuth", None), P("polar", "azimuth", None)),
        check_vma=False,
    )
```

time: 662 us -> 664 us (level)
  the two profiles are of different devices: /device:TPU:1 before, /device:TPU:17 now
where the time goes in v2:
time: 664 us; the launch traced here: 662 us
  Pallas kernels  263 us (40%)
  waiting for transfers between devices  188 us (28%)
  blocking collectives  87.8 us (13%)
  local copies, waits for them, and re-layouts  62.2 us (9%)
  starting transfers between devices  47.2 us (7%)
  other arithmetic  12.5 us (2%)
    all_to_all x4, waiting for transfers between devices, to_grid(): swap(transform(grid_kernel, one.reshape(tall, slim, LANES), wave, shape))  112 us
    pallas_call x2, Pallas kernels, couple(): pl.pallas_call(couple_kernel, grid=(modes // step,), out_shape=[jax.Shape...  98.1 us
    pallas_call x6, Pallas kernels, transform(): pl.pallas_call(kernel, out_shape=jax.ShapeDtypeStruct(shape, field.dtype)...  93.8 us
    all_gather x1, blocking collectives, per_device(): filters = lax.all_gather(filters, 'azimuth', axis=3, tiled=True)  87.8 us
    all_to_all x2, waiting for transfers between devices, to_modes(): spread = swap(pack(field, pick, parts, fold))  56.2 us
    pallas_call x2, Pallas kernels, mix_last(): pl.pallas_call(mix_kernel, grid=(slim,), out_shape=jax.ShapeDtypeStruct((...  51.3 us
    unnamed x70, local copies, waits for them, and re-layouts  35.9 us
    all_to_all x4, starting transfers between devices, to_grid(): swap(transform(grid_kernel, one.reshape(tall, slim, LANES), wave, shape))  21.3 us
  transfers between devices with their start and end apart: 10, of which 6 were waited for; matrix products, arithmetic and copies ran while one was open for 6% of the time, Pallas kernels for 31%

profile of v2, /device:TPU:17, one launch (start us, length us, event | category | flops | bytes accessed | tf_op | source)
XLA Modules:
  0.0 661.6 jit_solution(6133354607760852637)
XLA Ops:
  0.8 2.8 copy-done.2
  3.6 9.7 %shard_map.110 = bf16[4,32,192,128]{3,2,1,0:T(8,128)(2,1)S(1)} custom-call(bf16[2,32,192,256]{3,2,1,0:T(8,128)(2,1)S(1)} %bitcast.128, bf16[512,512]{1,0:T(8,128)(2,1)S(1)} %fusion.9.pick_ref), custom_call_target="tpu_custom_call" | custom-call | flops 3221225472 | bytes 12582912 | tf_op jit(solution)/shard_map/pallas_call | solution.py:37
  13.3 2.7 copy-done.1
  16.0 5.3 all-to-all-start.3
  21.3 4.8 sine_negate_fusion
  27.7 2.8 copy.173
  30.6 3.9 reshape.310
  34.5 56.2 %all-to-all-done.3.field_ref = bf16[4,32,192,128]{3,2,1,0:T(8,128)(2,1)} async-done(((bf16[4,32,192,128]{3,2,1,0:T(8,128)(2,1)}), bf16[4,32,192,128]{3,2,1,0:T(8,128)(2,1)}, u32[]{:S(2)}, u32[]{:S(2)}) %all-to-all-start.3) | async-done | bytes 6291488 | tf_op jit(solution)/shard_map/all_to_all | solution.py:292
  91.9 20.4 %shard_map.111 = bf16[768,32,128]{2,1,0:T(8,128)(2,1)} custom-call(bf16[4,32,192,128]{3,2,1,0:T(8,128)(2,1)} %all-to-all-done.3.field_ref, bf16[768,768]{1,0:T(8,128)(2,1)S(1)} %bitcast.132), custom_call_target="tpu_custom_call" | custom-call | flops 4831838208 | bytes 12582912 | tf_op jit(solution)/shard_map/pallas_call | solution.py:143
  112.3 4.5 collective-permute-start.2
  116.8 1.9 collective-permute-start.3
  118.8 9.7 %shard_map.104 = bf16[4,32,192,128]{3,2,1,0:T(8,128)(2,1)S(1)} custom-call(bf16[2,32,192,256]{3,2,1,0:T(8,128)(2,1)S(1)} %bitcast.131, bf16[512,512]{1,0:T(8,128)(2,1)S(1)} %fusion.9.pick_ref), custom_call_target="tpu_custom_call" | custom-call | flops 3221225472 | bytes 12582912 | tf_op jit(solution)/shard_map/pallas_call | solution.py:37
  128.5 2.7 copy-done
  131.2 5.4 all-to-all-start
  138.0 87.8 %all_gather.3 = f32[8,6,2,384]{0,2,1,3:T(2,128)S(1)} all-gather(f32[8,6,2,96]{0,2,1,3:T(2,128)S(1)} %copy.158), channel_id=1, replica_groups=mesh['polar'=8,'azimuth'=4] {'azimuth'}, dimensions={3}, use_global_device_ids=true | all-gather | bytes 184320 | tf_op jit(solution)/shard_map/all_gather | solution.py:261
  235.2 2.5 fusion.3
  237.7 4.8 copy.142
  242.4 3.0 reshape.305
  246.9 49.1 %shard_map.112 = (bf16[384,64,128]{2,1,0:T(8,128)(2,1)S(1)}, bf16[384,64,128]{2,1,0:T(8,128)(2,1)S(1)}) custom-call(bf16[384,64,128]{2,1,0:T(8,128)(2,1)} %bitcast.31.own_ref, bf16[384,64,128]{2,1,0:T(8,128)(2,1)} %collective-permute-done.2.low_ref, bf16[384,64,128]{2,1,0:T(8,128)(2,1)} %collective-permute-done.3.high_ref, ...), custom_call_target="tpu_custom_call" | custom-call | flops 9663676416 | bytes 31457280 | tf_op jit(solution)/shard_map/pallas_call | solution.py:201
  296.0 2.7 copy-done.11
  298.7 13.3 %shard_map.114 = bf16[4,32,192,128]{3,2,1,0:T(8,128)(2,1)S(1)} custom-call(bf16[768,32,128]{2,1,0:T(8,128)(2,1)S(1)} %bitcast.138, bf16[768,768]{1,0:T(8,128)(2,1)S(1)} %copy-done.9), custom_call_target="tpu_custom_call" | custom-call | flops 4831838208 | bytes 12582912 | tf_op jit(solution)/shard_map/pallas_call | solution.py:143
  312.0 2.7 copy-done.5
  314.7 5.3 all-to-all-start.5
  320.0 20.3 %shard_map.105 = bf16[768,32,128]{2,1,0:T(8,128)(2,1)} custom-call(bf16[4,32,192,128]{3,2,1,0:T(8,128)(2,1)} %all-to-all-done.field_ref, bf16[768,768]{1,0:T(8,128)(2,1)S(1)} %bitcast.133), custom_call_target="tpu_custom_call" | custom-call | flops 4831838208 | bytes 12582912 | tf_op jit(solution)/shard_map/pallas_call | solution.py:143
  340.4 6.8 %collective-permute-start = (bf16[384,64,128]{2,1,0:T(8,128)(2,1)}, bf16[384,64,128]{2,1,0:T(8,128)(2,1)}, u32[]{:S(2)}, u32[]{:S(2)}) collective-permute-start(bf16[384,64,128]{2,1,0:T(8,128)(2,1)} %bitcast.3.own_ref), channel_id=1, source_target_pairs={{0,4},{4,8},{8,12},{12,16},{16,20},{20,24},{24,28},{1,5},{5,9},{9,... | collective-permute-start | bytes 18874376 | tf_op jit(solution)/shard_map/ppermute | solution.py:297
  347.2 1.9 collective-permute-start.1
  349.1 2.8 copy-done.12
  351.9 13.3 %shard_map.113 = bf16[4,32,192,128]{3,2,1,0:T(8,128)(2,1)S(1)} custom-call(bf16[768,32,128]{2,1,0:T(8,128)(2,1)S(1)} %bitcast.136, bf16[768,768]{1,0:T(8,128)(2,1)S(1)} %copy-done.10), custom_call_target="tpu_custom_call" | custom-call | flops 4831838208 | bytes 12582912 | tf_op jit(solution)/shard_map/pallas_call | solution.py:143
  365.2 2.7 copy-done.3
  367.9 21.4 %all-to-all-done.5.refs_1_ = bf16[4,32,192,128]{3,2,1,0:T(8,128)(2,1)} async-done(((bf16[4,32,192,128]{3,2,1,0:T(8,128)(2,1)}), bf16[4,32,192,128]{3,2,1,0:T(8,128)(2,1)}, u32[]{:S(2)}, u32[]{:S(2)}) %all-to-all-start.5) | async-done | bytes 6291488 | tf_op jit(solution)/shard_map/all_to_all | solution.py:304
  389.3 5.3 all-to-all-start.4
  397.2 1.9 copy.172.gains_ref
  400.3 15.0 %collective-permute-done.low_ref = bf16[384,64,128]{2,1,0:T(8,128)(2,1)} collective-permute-done((bf16[384,64,128]{2,1,0:T(8,128)(2,1)}, bf16[384,64,128]{2,1,0:T(8,128)(2,1)}, u32[]{:S(2)}, u32[]{:S(2)}) %collective-permute-start) | collective-permute-done | bytes 6291488 | tf_op jit(solution)/shard_map/ppermute | solution.py:297
  415.4 4.7 collective-permute-done.1.high_ref
  420.1 49.0 %shard_map.106 = (bf16[384,64,128]{2,1,0:T(8,128)(2,1)S(1)}, bf16[384,64,128]{2,1,0:T(8,128)(2,1)S(1)}) custom-call(bf16[384,64,128]{2,1,0:T(8,128)(2,1)} %bitcast.3.own_ref, bf16[384,64,128]{2,1,0:T(8,128)(2,1)} %collective-permute-done.low_ref, bf16[384,64,128]{2,1,0:T(8,128)(2,1)} %collective-permute-done.1.high_ref, ...), custom_call_target="tpu_custom_call" | custom-call | flops 9663676416 | bytes 31457280 | tf_op jit(solution)/shard_map/pallas_call | solution.py:201
  469.1 2.7 copy-done.13
  471.8 13.3 %shard_map.108 = bf16[4,32,192,128]{3,2,1,0:T(8,128)(2,1)S(1)} custom-call(bf16[768,32,128]{2,1,0:T(8,128)(2,1)S(1)} %bitcast.139, bf16[768,768]{1,0:T(8,128)(2,1)S(1)} %copy.174.wave_ref), custom_call_target="tpu_custom_call" | custom-call | flops 4831838208 | bytes 12582912 | tf_op jit(solution)/shard_map/pallas_call | solution.py:143
  485.1 2.7 copy-done.6
  487.8 5.5 all-to-all-start.2
  493.2 2.8 copy-done.14
  496.0 13.3 %shard_map.107 = bf16[4,32,192,128]{3,2,1,0:T(8,128)(2,1)S(1)} custom-call(bf16[768,32,128]{2,1,0:T(8,128)(2,1)S(1)} %bitcast.137, bf16[768,768]{1,0:T(8,128)(2,1)S(1)} %copy.174.wave_ref), custom_call_target="tpu_custom_call" | custom-call | flops 4831838208 | bytes 12582912 | tf_op jit(solution)/shard_map/pallas_call | solution.py:143
  509.3 2.7 copy-done.4
  512.0 48.4 %all-to-all-done.2.refs_1_ = bf16[4,32,192,128]{3,2,1,0:T(8,128)(2,1)} async-done(((bf16[4,32,192,128]{3,2,1,0:T(8,128)(2,1)}), bf16[4,32,192,128]{3,2,1,0:T(8,128)(2,1)}, u32[]{:S(2)}, u32[]{:S(2)}) %all-to-all-start.2) | async-done | bytes 6291488 | tf_op jit(solution)/shard_map/all_to_all | solution.py:304
  560.5 5.2 all-to-all-start.1
  565.9 1.9 broadcast_multiply_fusion
  568.3 25.7 %shard_map.115 = bf16[2,32,192,256]{3,2,1,0:T(8,128)(2,1)} custom-call(bf16[4,32,192,128]{3,2,1,0:T(8,128)(2,1)} %all-to-all-done.4.refs_0_, bf16[4,32,192,128]{3,2,1,0:T(8,128)(2,1)} %all-to-all-done.5.refs_1_, bf16[1024,512]{1,0:T(8,128)(2,1)S(1)} %bitcast.135), custom_call_target="tpu_custom_call" | custom-call | flops 6442450944 | bytes 18874368 | tf_op jit(solution)/shard_map/pallas_call | solution.py:65
  594.0 42.1 %all-to-all-done.1.refs_0_ = bf16[4,32,192,128]{3,2,1,0:T(8,128)(2,1)} async-done(((bf16[4,32,192,128]{3,2,1,0:T(8,128)(2,1)}), bf16[4,32,192,128]{3,2,1,0:T(8,128)(2,1)}, u32[]{:S(2)}, u32[]{:S(2)}) %all-to-all-start.1) | async-done | bytes 6291488 | tf_op jit(solution)/shard_map/all_to_all | solution.py:304
  636.0 25.6 %shard_map.109 = bf16[2,32,192,256]{3,2,1,0:T(8,128)(2,1)} custom-call(bf16[4,32,192,128]{3,2,1,0:T(8,128)(2,1)} %all-to-all-done.1.refs_0_, bf16[4,32,192,128]{3,2,1,0:T(8,128)(2,1)} %all-to-all-done.2.refs_1_, bf16[1024,512]{1,0:T(8,128)(2,1)S(1)} %bitcast.134), custom_call_target="tpu_custom_call" | custom-call | flops 6442450944 | bytes 18874368 | tf_op jit(solution)/shard_map/pallas_call | solution.py:65
  (131 shorter events, 19.4 us)
Async XLA Ops:
  0.8 2.8 copy-start.2
  13.3 2.7 copy-start.1
  16.0 74.7 %all-to-all-start.3 = ((bf16[4,32,192,128]{3,2,1,0:T(8,128)(2,1)}), bf16[4,32,192,128]{3,2,1,0:T(8,128)(2,1)}, u32[]{:S(2)}, u32[]{:S(2)}) async-start(bf16[4,32,192,128]{3,2,1,0:T(8,128)(2,1)} %copy-done.1), calls=%async_computation.3 | async-start | bytes 12582912 | tf_op jit(solution)/shard_map/all_to_all | solution.py:292
  26.1 1.0 copy-start.15
  26.1 1.4 copy-start.17
  30.6 88.2 %slice-start = ((s8[6291456]{0:T(1024)(128)(4,1)}), s8[2097152]{0:T(1024)(128)(4,1)S(1)}, s32[]{:S(2)}) async-start(s8[6291456]{0:T(1024)(128)(4,1)} %bitcast.129), calls=%async_computation.6 | async-start | bytes 4194304
  90.6 1.3 copy-start.7
  91.9 26.9 %slice-start.1 = ((s8[6291456]{0:T(1024)(128)(4,1)}), s8[4194304]{0:T(1024)(128)(4,1)S(1)}, s32[]{:S(2)}) async-start(s8[6291456]{0:T(1024)(128)(4,1)} %bitcast.129), calls=%async_computation.7 | async-start | bytes 8388608
  112.3 134.6 %collective-permute-start.2 = (bf16[384,64,128]{2,1,0:T(8,128)(2,1)}, bf16[384,64,128]{2,1,0:T(8,128)(2,1)}, u32[]{:S(2)}, u32[]{:S(2)}) collective-permute-start(bf16[384,64,128]{2,1,0:T(8,128)(2,1)} %bitcast.31.own_ref), channel_id=1, source_target_pairs={{0,4},{4,8},{8,12},{12,16},{16,20},{20,24},{24,28},{1,5},{5,9},{9,... | collective-permute-start | bytes 18874376 | tf_op jit(solution)/shard_map/ppermute | solution.py:297
  116.8 130.1 %collective-permute-start.3 = (bf16[384,64,128]{2,1,0:T(8,128)(2,1)}, bf16[384,64,128]{2,1,0:T(8,128)(2,1)}, u32[]{:S(2)}, u32[]{:S(2)}) collective-permute-start(bf16[384,64,128]{2,1,0:T(8,128)(2,1)} %bitcast.31.own_ref), channel_id=1, source_target_pairs={{4,0},{8,4},{12,8},{16,12},{20,16},{24,20},{28,24},{5,1},{9,5},{13... | collective-permute-start | bytes 18874376 | tf_op jit(solution)/shard_map/ppermute | solution.py:298
  128.5 2.7 copy-start
  131.2 5.5 copy-start.26
  131.2 5.5 copy-start.27
  131.2 5.6 copy-start.29
  131.2 6.4 copy-start.21
  131.2 183.5 %all-to-all-start = ((bf16[4,32,192,128]{3,2,1,0:T(8,128)(2,1)}), bf16[4,32,192,128]{3,2,1,0:T(8,128)(2,1)}, u32[]{:S(2)}, u32[]{:S(2)}) async-start(bf16[4,32,192,128]{3,2,1,0:T(8,128)(2,1)} %copy-done), calls=%async_computation | async-start | bytes 12582912 | tf_op jit(solution)/shard_map/all_to_all | solution.py:292
  137.5 90.0 %copy-start.22 = (pred[8,3,2]{2,1,0:T(4,128)(4,1)}, pred[8,3,2]{2,1,0:T(4,128)(4,1)S(1)}, u32[]{:S(2)}) copy-start(pred[8,3,2]{2,1,0:T(4,128)(4,1)S(1)} %copy.152) | copy-start | bytes 148
  137.6 89.9 %copy-start.24 = (pred[8,3,2]{2,1,0:T(4,128)(4,1)}, pred[8,3,2]{2,1,0:T(4,128)(4,1)S(1)}, u32[]{:S(2)}) copy-start(pred[8,3,2]{2,1,0:T(4,128)(4,1)S(1)} %copy.154) | copy-start | bytes 148
  226.6 1.5 copy-start.28
  228.0 0.7 copy-start.20
  231.1 0.8 copy-start.23
  231.1 0.8 copy-start.25
  232.7 1.2 copy-start.18
  233.9 1.3 copy-start.16
  246.9 51.8 %copy-start.9 = (bf16[768,768]{1,0:T(8,128)(2,1)S(1)}, bf16[768,768]{1,0:T(8,128)(2,1)}, u32[]{:S(2)}) copy-start(bf16[768,768]{1,0:T(8,128)(2,1)} %copy.183.wave_ref) | copy-start | bytes 3538948
  296.0 2.7 copy-start.11
  312.0 2.7 copy-start.5
  314.7 74.6 %all-to-all-start.5 = ((bf16[4,32,192,128]{3,2,1,0:T(8,128)(2,1)}), bf16[4,32,192,128]{3,2,1,0:T(8,128)(2,1)}, u32[]{:S(2)}, u32[]{:S(2)}) async-start(bf16[4,32,192,128]{3,2,1,0:T(8,128)(2,1)} %copy-done.5), calls=%async_computation.5 | async-start | bytes 12582912 | tf_op jit(solution)/shard_map/all_to_all | solution.py:304
  320.0 29.1 %copy-start.10 = (bf16[768,768]{1,0:T(8,128)(2,1)S(1)}, bf16[768,768]{1,0:T(8,128)(2,1)}, u32[]{:S(2)}) copy-start(bf16[768,768]{1,0:T(8,128)(2,1)} %copy.183.wave_ref) | copy-start | bytes 3538948
  340.4 75.0 %collective-permute-start = (bf16[384,64,128]{2,1,0:T(8,128)(2,1)}, bf16[384,64,128]{2,1,0:T(8,128)(2,1)}, u32[]{:S(2)}, u32[]{:S(2)}) collective-permute-start(bf16[384,64,128]{2,1,0:T(8,128)(2,1)} %bitcast.3.own_ref), channel_id=1, source_target_pairs={{0,4},{4,8},{8,12},{12,16},{16,20},{20,24},{24,28},{1,5},{5,9},{9,... | collective-permute-start | bytes 18874376 | tf_op jit(solution)/shard_map/ppermute | solution.py:297
  347.2 72.9 %collective-permute-start.1 = (bf16[384,64,128]{2,1,0:T(8,128)(2,1)}, bf16[384,64,128]{2,1,0:T(8,128)(2,1)}, u32[]{:S(2)}, u32[]{:S(2)}) collective-permute-start(bf16[384,64,128]{2,1,0:T(8,128)(2,1)} %bitcast.3.own_ref), channel_id=1, source_target_pairs={{4,0},{8,4},{12,8},{16,12},{20,16},{24,20},{28,24},{5,1},{9,5},{13... | collective-permute-start | bytes 18874376 | tf_op jit(solution)/shard_map/ppermute | solution.py:298
  349.1 2.8 copy-start.12
  365.2 2.7 copy-start.3
  367.9 26.7 %copy-start.8 = (bf16[768,768]{0,1:T(8,128)(2,1)S(1)}, bf16[768,768]{0,1:T(8,128)(2,1)}, u32[]{:S(2)}) copy-start(bf16[768,768]{0,1:T(8,128)(2,1)} %reshape.310) | copy-start | bytes 3538948
  389.3 98.4 %all-to-all-start.4 = ((bf16[4,32,192,128]{3,2,1,0:T(8,128)(2,1)}), bf16[4,32,192,128]{3,2,1,0:T(8,128)(2,1)}, u32[]{:S(2)}, u32[]{:S(2)}) async-start(bf16[4,32,192,128]{3,2,1,0:T(8,128)(2,1)} %copy-done.3), calls=%async_computation.4 | async-start | bytes 12582912 | tf_op jit(solution)/shard_map/all_to_all | solution.py:304
  469.1 2.7 copy-start.13
  485.1 2.7 copy-start.6
  487.8 72.7 %all-to-all-start.2 = ((bf16[4,32,192,128]{3,2,1,0:T(8,128)(2,1)}), bf16[4,32,192,128]{3,2,1,0:T(8,128)(2,1)}, u32[]{:S(2)}, u32[]{:S(2)}) async-start(bf16[4,32,192,128]{3,2,1,0:T(8,128)(2,1)} %copy-done.6), calls=%async_computation.2 | async-start | bytes 12582912 | tf_op jit(solution)/shard_map/all_to_all | solution.py:304
  493.2 2.8 copy-start.14
  509.3 2.7 copy-start.4
  512.0 53.7 %copy-start.19 = (bf16[2,256,256]{2,1,0:T(8,128)(2,1)S(1)}, bf16[2,256,256]{2,1,0:T(8,128)(2,1)}, u32[]{:S(2)}) copy-start(bf16[2,256,256]{2,1,0:T(8,128)(2,1)} %param.11) | copy-start | bytes 786436
  560.5 75.6 %all-to-all-start.1 = ((bf16[4,32,192,128]{3,2,1,0:T(8,128)(2,1)}), bf16[4,32,192,128]{3,2,1,0:T(8,128)(2,1)}, u32[]{:S(2)}, u32[]{:S(2)}) async-start(bf16[4,32,192,128]{3,2,1,0:T(8,128)(2,1)} %copy-done.4), calls=%async_computation.1 | async-start | bytes 12582912 | tf_op jit(solution)/shard_map/all_to_all | solution.py:304

commit v3 on v2

--- a/solution.py
+++ b/solution.py
@@ -10,6 +10,7 @@
 
 K = 2
 LANES = 128
+STEP = 4
 
 
 def spectral_tables(nlon, modes):
@@ -23,12 +24,13 @@
 
 
 def pack_kernel(field_ref, pick_ref, out_ref):
-    fold = field_ref.shape[0]
+    fold, step, width, channels = field_ref.shape
     parts, _, _, lanes = out_ref.shape
-    wide = jnp.concatenate([field_ref[h, 0] for h in range(fold)], axis=1)
+    wide = jnp.concatenate([field_ref[h].reshape(step * width, channels) for h in range(fold)], axis=1)
     packed = jnp.dot(wide, pick_ref[...], preferred_element_type=jnp.float32)
     for g in range(parts):
-        out_ref[g, 0] = packed[:, g * lanes : (g + 1) * lanes].astype(out_ref.dtype)
+        piece = packed[:, g * lanes : (g + 1) * lanes].astype(out_ref.dtype)
+        out_ref[g] = piece.reshape(step, width, lanes)
 
 
 def pack(field, pick, parts, fold):
@@ -36,14 +38,14 @@
     slim = rows // fold
     return pl.pallas_call(
         pack_kernel,
-        grid=(slim,),
+        grid=(slim // STEP,),
         out_shape=jax.ShapeDtypeStruct((parts, slim, width, LANES), field.dtype),
         in_specs=[
-            pl.BlockSpec((fold, 1, width, channels), lambda i: (0, i, 0, 0)),
+            pl.BlockSpec((fold, STEP, width, channels), lambda i: (0, i, 0, 0)),
             pl.BlockSpec(pick.shape, lambda i: (0, 0)),
         ],
-        out_specs=pl.BlockSpec((parts, 1, width, LANES), lambda i: (0, i, 0, 0)),
-        compiler_params=pltpu.CompilerParams(vmem_limit_bytes=16 * 2**20),
+        out_specs=pl.BlockSpec((parts, STEP, width, LANES), lambda i: (0, i, 0, 0)),
+        compiler_params=pltpu.CompilerParams(vmem_limit_bytes=32 * 2**20),
         cost_estimate=pl.CostEstimate(
             flops=2 * field.size * parts * LANES, bytes_accessed=4 * field.size, transcendentals=0
         ),
@@ -52,11 +54,15 @@
 
 def mix_kernel(*refs):
     mix_ref, out_ref = refs[K:]
-    fold, _, _, channels = out_ref.shape
-    wide = jnp.concatenate([ref[g, 0] for ref in refs[:K] for g in range(refs[0].shape[0])], axis=1)
+    fold, step, width, channels = out_ref.shape
+    parts, _, _, lanes = refs[0].shape
+    wide = jnp.concatenate(
+        [ref[g].reshape(step * width, lanes) for ref in refs[:K] for g in range(parts)], axis=1
+    )
     mixed = jnp.dot(wide, mix_ref[...], preferred_element_type=jnp.float32)
     for h in range(fold):
-        out_ref[h, 0] = mixed[:, h * channels : (h + 1) * channels].astype(out_ref.dtype)
+        piece = mixed[:, h * channels : (h + 1) * channels].astype(out_ref.dtype)
+        out_ref[h] = piece.reshape(step, width, channels)
 
 
 def mix_last(fields, mix, fold):
@@ -64,12 +70,12 @@
     channels = mix.shape[1] // fold
     out = pl.pallas_call(
         mix_kernel,
-        grid=(slim,),
+        grid=(slim // STEP,),
         out_shape=jax.ShapeDtypeStruct((fold, slim, width, channels), fields[0].dtype),
-        in_specs=[pl.BlockSpec((parts, 1, width, lanes), lambda i: (0, i, 0, 0))] * K
+        in_specs=[pl.BlockSpec((parts, STEP, width, lanes), lambda i: (0, i, 0, 0))] * K
         + [pl.BlockSpec(mix.shape, lambda i: (0, 0))],
-        out_specs=pl.BlockSpec((fold, 1, width, channels), lambda i: (0, i, 0, 0)),
-        compiler_params=pltpu.CompilerParams(vmem_limit_bytes=16 * 2**20),
+        out_specs=pl.BlockSpec((fold, STEP, width, channels), lambda i: (0, i, 0, 0)),
+        compiler_params=pltpu.CompilerParams(vmem_limit_bytes=32 * 2**20),
         cost_estimate=pl.CostEstimate(
             flops=2 * slim * width * mix.size, bytes_accessed=6 * fields[0].size, transcendentals=0
         ),
@@ -259,6 +265,7 @@
     fold = LANES // share
     slim = rows // fold
     filters = lax.all_gather(filters, "azimuth", axis=3, tiled=True)
+    filters, signal = lax.optimization_barrier((filters, signal))
     modes = filters.shape[3]
     forward, inverse = spectral_tables(width * parts, modes)
 
@@ -288,8 +295,7 @@
     def by_wave(wave):
         return jnp.swapaxes(wave, 1, 2).reshape(parts * width, tall)
 
-    def to_modes(field, wave):
-        spread = swap(pack(field, pick, parts, fold))
+    def to_modes(spread, wave):
         spectra = transform(modes_kernel, spread, jnp.transpose(by_wave(wave)), (tall, slim, LANES))
         return spectra.reshape(modes, 2 * slim, LANES)
 
@@ -303,9 +309,12 @@
         shape = (parts, slim, width, LANES)
         return [swap(transform(grid_kernel, one.reshape(tall, slim, LANES), wave, shape)) for one in sums]
 
-    first = to_modes(signal, forward)
-    second = to_modes(cotangent, inverse)
+    first = swap(pack(signal, pick, parts, fold))
+    first, second = lax.optimization_barrier((first, pack(cotangent, pick, parts, fold)))
+    first = to_modes(first, forward)
     first_halo = halo(first)
+    second = to_modes(swap(second), inverse)
+    first, second = lax.optimization_barrier((first, second))
     second_halo = halo(second)
     sums = couple(first, *first_halo, weave, table)
     back_sums = couple(second, *second_halo, back_weave, back_table)

time: 664 us -> 625 us (0.941)
  the two profiles are of different devices: /device:TPU:17 before, /device:TPU:1 now
where the time goes in v3:
time: 625 us; the launch traced here: 621 us
  Pallas kernels  225 us (36%)
  waiting for transfers between devices  220 us (35%)
  local copies, waits for them, and re-layouts  87.6 us (14%)
  starting transfers between devices  46.3 us (7%)
  blocking collectives  25.2 us (4%)
  other arithmetic  16.3 us (3%)
    all_to_all x4, waiting for transfers between devices, to_grid(): swap(transform(grid_kernel, one.reshape(tall, slim, LANES), wave, shape))  149 us
    pallas_call x2, Pallas kernels, couple(): pl.pallas_call(couple_kernel, grid=(modes // step,), out_shape=[jax.Shape...  98 us
    pallas_call x6, Pallas kernels, transform(): pl.pallas_call(kernel, out_shape=jax.ShapeDtypeStruct(shape, field.dtype)...  91 us
    all_to_all x1, waiting for transfers between devices, per_device(): first = swap(pack(signal, pick, parts, fold))  44.4 us
    unnamed x52, local copies, waits for them, and re-layouts  40.9 us
    all_to_all x1, waiting for transfers between devices, per_device(): second = to_modes(swap(second), inverse)  26.9 us
    all_gather x1, blocking collectives, per_device(): filters = lax.all_gather(filters, 'azimuth', axis=3, tiled=True)  25.2 us
    pallas_call x2, Pallas kernels, mix_last(): pl.pallas_call(mix_kernel, grid=(slim // STEP,), out_shape=jax.ShapeDtype...  25.1 us
  transfers between devices with their start and end apart: 10, of which 5 were waited for; matrix products, arithmetic and copies ran while one was open for 10% of the time, Pallas kernels for 20%

profile of v3, /device:TPU:1, one launch (start us, length us, event | category | flops | bytes accessed | tf_op | source)
XLA Modules:
  0.0 621.5 jit_solution(8291090992651087412)
XLA Ops:
  1.8 25.2 %all_gather.3 = f32[8,6,2,384]{0,2,1,3:T(2,128)} all-gather(f32[8,6,2,96]{0,2,1,3:T(2,128)S(1)} %copy.140), channel_id=1, replica_groups=mesh['polar'=8,'azimuth'=4] {'azimuth'}, dimensions={3}, use_global_device_ids=true | all-gather | bytes 184320 | tf_op jit(solution)/shard_map/all_gather | solution.py:267
  27.1 2.8 copy-done.2
  29.9 5.4 shard_map.104
  35.3 2.7 copy-done.1
  38.0 5.3 all-to-all-start
  43.3 4.8 sine_negate_fusion
  49.5 4.8 copy.141
  54.3 3.0 reshape.306
  57.3 2.8 copy-done.3
  60.0 5.4 shard_map.105
  65.4 2.7 copy-done
  68.1 44.4 %all-to-all-done.field_ref = bf16[4,32,192,128]{3,2,1,0:T(8,128)(2,1)} async-done(((bf16[4,32,192,128]{3,2,1,0:T(8,128)(2,1)}), bf16[4,32,192,128]{3,2,1,0:T(8,128)(2,1)}, u32[]{:S(2)}, u32[]{:S(2)}) %all-to-all-start) | async-done | bytes 6291488 | tf_op jit(solution)/shard_map/all_to_all | solution.py:312
  112.6 20.2 %shard_map.106 = bf16[768,32,128]{2,1,0:T(8,128)(2,1)} custom-call(bf16[4,32,192,128]{3,2,1,0:T(8,128)(2,1)} %all-to-all-done.field_ref, bf16[768,768]{1,0:T(8,128)(2,1)S(1)} %bitcast.130), custom_call_target="tpu_custom_call" | custom-call | flops 4831838208 | bytes 12582912 | tf_op jit(solution)/shard_map/pallas_call | solution.py:149
  132.8 4.6 collective-permute-start
  137.4 2.8 collective-permute-start.1
  140.2 5.4 all-to-all-start.1
  145.7 2.8 slice_bitcast_fusion.5
  171.1 4.8 copy.142
  175.8 3.0 reshape.308
  181.5 2.7 copy.171.gains_ref
  188.7 26.9 %all-to-all-done.1.field_ref = bf16[4,32,192,128]{3,2,1,0:T(8,128)(2,1)} async-done(((bf16[4,32,192,128]{3,2,1,0:T(8,128)(2,1)}), bf16[4,32,192,128]{3,2,1,0:T(8,128)(2,1)}, u32[]{:S(2)}, u32[]{:S(2)}) %all-to-all-start.1) | async-done | bytes 6291488 | tf_op jit(solution)/shard_map/all_to_all | solution.py:316
  215.6 17.7 %shard_map.107 = bf16[768,32,128]{2,1,0:T(8,128)(2,1)S(1)} custom-call(bf16[4,32,192,128]{3,2,1,0:T(8,128)(2,1)} %all-to-all-done.1.field_ref, bf16[768,768]{1,0:T(8,128)(2,1)S(1)} %bitcast.131), custom_call_target="tpu_custom_call" | custom-call | flops 4831838208 | bytes 12582912 | tf_op jit(solution)/shard_map/pallas_call | solution.py:149
  235.9 49.1 %shard_map.108 = (bf16[384,64,128]{2,1,0:T(8,128)(2,1)S(1)}, bf16[384,64,128]{2,1,0:T(8,128)(2,1)S(1)}) custom-call(bf16[384,64,128]{2,1,0:T(8,128)(2,1)} %bitcast.4.own_ref, bf16[384,64,128]{2,1,0:T(8,128)(2,1)} %collective-permute-done.low_ref, bf16[384,64,128]{2,1,0:T(8,128)(2,1)} %collective-permute-done.1.high_ref, ...), custom_call_target="tpu_custom_call" | custom-call | flops 9663676416 | bytes 31457280 | tf_op jit(solution)/shard_map/pallas_call | solution.py:207
  285.0 2.7 copy-done.12
  287.7 13.3 %shard_map.110 = bf16[4,32,192,128]{3,2,1,0:T(8,128)(2,1)S(1)} custom-call(bf16[768,32,128]{2,1,0:T(8,128)(2,1)S(1)} %bitcast.139, bf16[768,768]{1,0:T(8,128)(2,1)S(1)} %copy-done.9), custom_call_target="tpu_custom_call" | custom-call | flops 4831838208 | bytes 12582912 | tf_op jit(solution)/shard_map/pallas_call | solution.py:149
  301.0 2.7 copy-done.6
  303.7 5.3 all-to-all-start.3
  309.0 2.9 collective-permute-start.2
  311.9 4.0 collective-permute-start.3
  316.0 2.8 copy-done.13
  318.7 13.3 %shard_map.109 = bf16[4,32,192,128]{3,2,1,0:T(8,128)(2,1)S(1)} custom-call(bf16[768,32,128]{2,1,0:T(8,128)(2,1)S(1)} %bitcast.137, bf16[768,768]{1,0:T(8,128)(2,1)S(1)} %copy-done.9), custom_call_target="tpu_custom_call" | custom-call | flops 4831838208 | bytes 12582912 | tf_op jit(solution)/shard_map/pallas_call | solution.py:149
  332.0 2.7 copy-done.4
  334.7 43.8 %all-to-all-done.3.refs_1_ = bf16[4,32,192,128]{3,2,1,0:T(8,128)(2,1)} async-done(((bf16[4,32,192,128]{3,2,1,0:T(8,128)(2,1)}), bf16[4,32,192,128]{3,2,1,0:T(8,128)(2,1)}, u32[]{:S(2)}, u32[]{:S(2)}) %all-to-all-start.3) | async-done | bytes 6291488 | tf_op jit(solution)/shard_map/all_to_all | solution.py:310
  378.6 5.3 all-to-all-start.2
  389.3 2.8 copy-done.11
  392.1 48.9 %shard_map.112 = (bf16[384,64,128]{2,1,0:T(8,128)(2,1)S(1)}, bf16[384,64,128]{2,1,0:T(8,128)(2,1)S(1)}) custom-call(bf16[384,64,128]{2,1,0:T(8,128)(2,1)S(1)} %bitcast.136, bf16[384,64,128]{2,1,0:T(8,128)(2,1)} %collective-permute-done.2.low_ref, bf16[384,64,128]{2,1,0:T(8,128)(2,1)} %collective-permute-done.3.high_ref, ...), custom_call_target="tpu_custom_call" | custom-call | flops 9663676416 | bytes 31457280 | tf_op jit(solution)/shard_map/pallas_call | solution.py:207
  441.0 2.7 copy-done.14
  443.7 13.3 %shard_map.114 = bf16[4,32,192,128]{3,2,1,0:T(8,128)(2,1)S(1)} custom-call(bf16[768,32,128]{2,1,0:T(8,128)(2,1)S(1)} %bitcast.140, bf16[768,768]{1,0:T(8,128)(2,1)S(1)} %copy.181.wave_ref), custom_call_target="tpu_custom_call" | custom-call | flops 4831838208 | bytes 12582912 | tf_op jit(solution)/shard_map/pallas_call | solution.py:149
  457.0 2.7 copy-done.7
  459.6 5.4 all-to-all-start.5
  465.1 2.8 copy-done.15
  467.9 13.3 %shard_map.113 = bf16[4,32,192,128]{3,2,1,0:T(8,128)(2,1)S(1)} custom-call(bf16[768,32,128]{2,1,0:T(8,128)(2,1)S(1)} %bitcast.138, bf16[768,768]{1,0:T(8,128)(2,1)S(1)} %copy.181.wave_ref), custom_call_target="tpu_custom_call" | custom-call | flops 4831838208 | bytes 12582912 | tf_op jit(solution)/shard_map/pallas_call | solution.py:149
  481.2 2.7 copy-done.5
  483.9 50.5 %all-to-all-done.5.refs_1_ = bf16[4,32,192,128]{3,2,1,0:T(8,128)(2,1)} async-done(((bf16[4,32,192,128]{3,2,1,0:T(8,128)(2,1)}), bf16[4,32,192,128]{3,2,1,0:T(8,128)(2,1)}, u32[]{:S(2)}, u32[]{:S(2)}) %all-to-all-start.5) | async-done | bytes 6291488 | tf_op jit(solution)/shard_map/all_to_all | solution.py:310
  534.4 5.2 all-to-all-start.4
  542.2 12.5 %shard_map.111 = bf16[2,32,192,256]{3,2,1,0:T(8,128)(2,1)} custom-call(bf16[4,32,192,128]{3,2,1,0:T(8,128)(2,1)} %all-to-all-done.2.refs_0_, bf16[4,32,192,128]{3,2,1,0:T(8,128)(2,1)} %all-to-all-done.3.refs_1_, bf16[1024,512]{1,0:T(8,128)(2,1)S(1)} %bitcast.133), custom_call_target="tpu_custom_call" | custom-call | flops 6442450944 | bytes 18874368 | tf_op jit(solution)/shard_map/pallas_call | solution.py:71
  554.7 54.2 %all-to-all-done.4.refs_0_ = bf16[4,32,192,128]{3,2,1,0:T(8,128)(2,1)} async-done(((bf16[4,32,192,128]{3,2,1,0:T(8,128)(2,1)}), bf16[4,32,192,128]{3,2,1,0:T(8,128)(2,1)}, u32[]{:S(2)}, u32[]{:S(2)}) %all-to-all-start.4) | async-done | bytes 6291488 | tf_op jit(solution)/shard_map/all_to_all | solution.py:310
  609.0 12.5 %shard_map.115 = bf16[2,32,192,256]{3,2,1,0:T(8,128)(2,1)} custom-call(bf16[4,32,192,128]{3,2,1,0:T(8,128)(2,1)} %all-to-all-done.4.refs_0_, bf16[4,32,192,128]{3,2,1,0:T(8,128)(2,1)} %all-to-all-done.5.refs_1_, bf16[1024,512]{1,0:T(8,128)(2,1)S(1)} %bitcast.132), custom_call_target="tpu_custom_call" | custom-call | flops 6442450944 | bytes 18874368 | tf_op jit(solution)/shard_map/pallas_call | solution.py:71
  (112 shorter events, 42.9 us)
Async XLA Ops:
  27.1 2.8 copy-start.2
  35.3 2.7 copy-start.1
  38.0 74.6 %all-to-all-start = ((bf16[4,32,192,128]{3,2,1,0:T(8,128)(2,1)}), bf16[4,32,192,128]{3,2,1,0:T(8,128)(2,1)}, u32[]{:S(2)}, u32[]{:S(2)}) async-start(bf16[4,32,192,128]{3,2,1,0:T(8,128)(2,1)} %copy-done.1), calls=%async_computation | async-start | bytes 12582912 | tf_op jit(solution)/shard_map/all_to_all | solution.py:312
  48.1 1.5 copy-start.16
  57.3 2.8 copy-start.3
  65.4 2.7 copy-start
  132.8 103.0 %collective-permute-start = (bf16[384,64,128]{2,1,0:T(8,128)(2,1)}, bf16[384,64,128]{2,1,0:T(8,128)(2,1)}, u32[]{:S(2)}, u32[]{:S(2)}) collective-permute-start(bf16[384,64,128]{2,1,0:T(8,128)(2,1)} %bitcast.4.own_ref), channel_id=1, source_target_pairs={{0,4},{4,8},{8,12},{12,16},{16,20},{20,24},{24,28},{1,5},{5,9},{9,... | collective-permute-start | bytes 18874376 | tf_op jit(solution)/shard_map/ppermute | solution.py:303
  137.4 98.4 %collective-permute-start.1 = (bf16[384,64,128]{2,1,0:T(8,128)(2,1)}, bf16[384,64,128]{2,1,0:T(8,128)(2,1)}, u32[]{:S(2)}, u32[]{:S(2)}) collective-permute-start(bf16[384,64,128]{2,1,0:T(8,128)(2,1)} %bitcast.4.own_ref), channel_id=1, source_target_pairs={{4,0},{8,4},{12,8},{16,12},{20,16},{24,20},{28,24},{5,1},{9,5},{13... | collective-permute-start | bytes 18874376 | tf_op jit(solution)/shard_map/ppermute | solution.py:304
  140.2 75.4 %all-to-all-start.1 = ((bf16[4,32,192,128]{3,2,1,0:T(8,128)(2,1)}), bf16[4,32,192,128]{3,2,1,0:T(8,128)(2,1)}, u32[]{:S(2)}, u32[]{:S(2)}) async-start(bf16[4,32,192,128]{3,2,1,0:T(8,128)(2,1)} %copy-done), calls=%async_computation.1 | async-start | bytes 12582912 | tf_op jit(solution)/shard_map/all_to_all | solution.py:316
  148.4 8.5 %copy-start.19 = (s32[8,6]{1,0:T(8,128)S(1)}, s32[8,6]{1,0:T(8,128)}, u32[]{:S(2)}) copy-start(s32[8,6]{1,0:T(8,128)} %param.16) | copy-start | bytes 580
  148.4 8.5 %copy-start.20 = (s32[8,6]{1,0:T(8,128)S(1)}, s32[8,6]{1,0:T(8,128)}, u32[]{:S(2)}) copy-start(s32[8,6]{1,0:T(8,128)} %param.15) | copy-start | bytes 580
  148.4 8.5 %copy-start.22 = (s32[8]{0:T(128)S(1)}, s32[8]{0:T(128)}, u32[]{:S(2)}) copy-start(s32[8]{0:T(128)} %param.14) | copy-start | bytes 100
  185.9 1.1 copy-start.17
  215.6 20.3 %copy-start.8 = (f32[384,4,192]{2,1,0:T(4,128)S(1)}, f32[384,4,192]{2,1,0:T(4,128)}, u32[]{:S(2)}) copy-start(f32[384,4,192]{2,1,0:T(4,128)} %copy.171.gains_ref) | copy-start | bytes 3538948
  233.2 2.6 copy-start.10
  235.9 51.9 %copy-start.9 = (bf16[768,768]{1,0:T(8,128)(2,1)S(1)}, bf16[768,768]{1,0:T(8,128)(2,1)}, u32[]{:S(2)}) copy-start(bf16[768,768]{1,0:T(8,128)(2,1)} %copy.172.wave_ref) | copy-start | bytes 3538948
  285.0 2.7 copy-start.12
  301.0 2.7 copy-start.6
  303.7 74.9 %all-to-all-start.3 = ((bf16[4,32,192,128]{3,2,1,0:T(8,128)(2,1)}), bf16[4,32,192,128]{3,2,1,0:T(8,128)(2,1)}, u32[]{:S(2)}, u32[]{:S(2)}) async-start(bf16[4,32,192,128]{3,2,1,0:T(8,128)(2,1)} %copy-done.6), calls=%async_computation.3 | async-start | bytes 12582912 | tf_op jit(solution)/shard_map/all_to_all | solution.py:310
  309.0 80.3 %collective-permute-start.2 = (bf16[384,64,128]{2,1,0:T(8,128)(2,1)}, bf16[384,64,128]{2,1,0:T(8,128)(2,1)}, u32[]{:S(2)}, u32[]{:S(2)}) collective-permute-start(bf16[384,64,128]{2,1,0:T(8,128)(2,1)} %bitcast.134), channel_id=1, source_target_pairs={{0,4},{4,8},{8,12},{12,16},{16,20},{20,24},{24,28},{1,5},{5,9},{9,... | collective-permute-start | bytes 18874376 | tf_op jit(solution)/shard_map/ppermute | solution.py:303
  311.9 77.4 %collective-permute-start.3 = (bf16[384,64,128]{2,1,0:T(8,128)(2,1)}, bf16[384,64,128]{2,1,0:T(8,128)(2,1)}, u32[]{:S(2)}, u32[]{:S(2)}) collective-permute-start(bf16[384,64,128]{2,1,0:T(8,128)(2,1)} %bitcast.135), channel_id=1, source_target_pairs={{4,0},{8,4},{12,8},{16,12},{20,16},{24,20},{28,24},{5,1},{9,5},{13... | collective-permute-start | bytes 18874376 | tf_op jit(solution)/shard_map/ppermute | solution.py:304
  316.0 2.8 copy-start.13
  332.0 2.7 copy-start.4
  378.6 81.1 %all-to-all-start.2 = ((bf16[4,32,192,128]{3,2,1,0:T(8,128)(2,1)}), bf16[4,32,192,128]{3,2,1,0:T(8,128)(2,1)}, u32[]{:S(2)}, u32[]{:S(2)}) async-start(bf16[4,32,192,128]{3,2,1,0:T(8,128)(2,1)} %copy-done.4), calls=%async_computation.2 | async-start | bytes 12582912 | tf_op jit(solution)/shard_map/all_to_all | solution.py:310
  383.9 0.7 copy-start.21
  389.3 2.8 copy-start.11
  441.0 2.7 copy-start.14
  456.9 2.7 copy-start.7
  459.6 74.8 %all-to-all-start.5 = ((bf16[4,32,192,128]{3,2,1,0:T(8,128)(2,1)}), bf16[4,32,192,128]{3,2,1,0:T(8,128)(2,1)}, u32[]{:S(2)}, u32[]{:S(2)}) async-start(bf16[4,32,192,128]{3,2,1,0:T(8,128)(2,1)} %copy-done.7), calls=%async_computation.5 | async-start | bytes 12582912 | tf_op jit(solution)/shard_map/all_to_all | solution.py:310
  465.1 2.8 copy-start.15
  481.2 2.7 copy-start.5
  483.9 55.8 %copy-start.18 = (bf16[2,256,256]{2,1,0:T(8,128)(2,1)S(1)}, bf16[2,256,256]{2,1,0:T(8,128)(2,1)}, u32[]{:S(2)}) copy-start(bf16[2,256,256]{2,1,0:T(8,128)(2,1)} %param.11) | copy-start | bytes 786436
  534.4 74.6 %all-to-all-start.4 = ((bf16[4,32,192,128]{3,2,1,0:T(8,128)(2,1)}), bf16[4,32,192,128]{3,2,1,0:T(8,128)(2,1)}, u32[]{:S(2)}, u32[]{:S(2)}) async-start(bf16[4,32,192,128]{3,2,1,0:T(8,128)(2,1)} %copy-done.5), calls=%async_computation.4 | async-start | bytes 12582912 | tf_op jit(solution)/shard_map/all_to_all | solution.py:310
